TPU v7x, 32 devices: a whole 2x2x4 slice. The times are simulated.
32 devices in a mesh: grp: 4 (over y, x), row: 8 (over z, core).
Axes of the slice: x: 2, y: 2, z: 4, core: 2. Of those that a mesh axis runs over, the one named last changes fastest.
Arguments:
- tokens: bfloat16 [768, 20480], P('grp', 'row'), may hold values from -11 to 11
- segments: int32 [40, 512], P('row'), may hold values from 0 to 3, never falling along the last dimension, each value on 1 to 256 neighbouring positions
- owners: int32 [12], replicated, may hold values from 0 to 7, as said below
- masters: float32 [4, 64, 36864], P('grp', 'row'), may hold values from -4 to 4
- first_moment: float32 [4, 64, 36864], P('grp', 'row'), may hold values from -429.32505 to 429.32505
- second_moment: float32 [4, 64, 36864], P('grp', 'row'), may hold values from 0 to 20480
- vectors: float32 [2, 12, 768], P(None, None, 'grp'), may hold values from -3 to 3
- vector_first: float32 [2, 12, 768], P(None, None, 'grp'), may hold values from -429.32505 to 429.32505
- vector_second: float32 [2, 12, 768], P(None, None, 'grp'), may hold values from 0 to 20480
- cotangent: float32 [768, 20480], P('grp', 'row'), may hold values from -6 to 6
Outputs:
- layer_output: float32 [768, 20480], P('grp', 'row')
- input_grad: float32 [768, 20480], P('grp', 'row')
- new_masters: float32 [4, 64, 36864], P('grp', 'row')
- new_first: float32 [4, 64, 36864], P('grp', 'row')
- new_second: float32 [4, 64, 36864], P('grp', 'row')
- new_vectors: float32 [2, 12, 768], P(None, None, 'grp')
- new_vector_first: float32 [2, 12, 768], P(None, None, 'grp')
- new_vector_second: float32 [2, 12, 768], P(None, None, 'grp')
Inputs may be any that keep to these rules, and one draw needn't show every extreme that they name: `owners`: each matrix is owned whole by one index of row. The matrices of 4 blocks go two to a device, on distinct devices, which then own exactly 8 blocks; each matrix of one block goes to another device, no device owning more than 8 blocks.
All inputs are finite; a program needn't handle non-finite values.
Results may differ from a plain program's by a relative error of at most 0.03.
The roundings to bfloat16 on the way count: a program that leaves them out, or rounds other values in their place, can miss the bound.
Values may be sent and summed in bfloat16 or wider, within the bound.
No kernel may reach another device: no remote copies, remote signals or barrier semaphores. Data moves between devices by JAX's collectives and lax.ppermute only.
A program may use at most 192 MiB of HBM per device.

v0:
```python
import jax
import jax.numpy as jnp
import numpy as np
from jax import lax
from jax.sharding import PartitionSpec as P

HEADS = 12
LAYERS = 2
STEP = 7


BETA_ONE = 0.9
BETA_TWO = 0.999
LEARN_RATE = 0.1
VECTOR_RATE = 0.5
WEIGHT_DECAY = 0.01
ADAM_EPSILON = 1e-08
NORM_EPSILON = 1e-12
MASK_FILL = -1e30
FULL_PRECISION = lax.Precision.HIGHEST


def block_layout(groups, layers):
    counts = []
    block_matrix = []
    block_step = []
    for layer_index in range(layers):
        for matrix_type in range(6):
            amount = 1 if matrix_type < 3 else groups
            for position in range(amount):
                block_matrix.append(layer_index * 6 + matrix_type)
                block_step.append(position)
            counts.append(amount)
    return (
        np.array(counts, np.int32),
        np.array(block_matrix, np.int32),
        np.array(block_step, np.int32),
    )


def slot_index(owners, groups, layers, capacity):
    counts, block_matrix, block_step = block_layout(groups, layers)
    matrix_ids = jnp.arange(counts.shape[0], dtype=jnp.int32)
    same_owner = owners[:, None] == owners[None, :]
    earlier = matrix_ids[None, :] < matrix_ids[:, None]
    slot_of = jnp.sum(
        jnp.where(same_owner & earlier, jnp.asarray(counts, jnp.int32)[None, :], 0), axis=1
    )
    starts = owners * capacity + slot_of
    choose = (jnp.asarray(block_matrix, jnp.int32)[:, None] == matrix_ids[None, :]).astype(
        jnp.int32
    )
    block_index = jnp.sum(choose * starts[None, :], axis=1) + jnp.asarray(block_step, jnp.int32)
    return (block_index, slot_of)


def exact_gelu(values):
    return jax.nn.gelu(values, approximate=False)


def normalize(resid, gain_row, bias_row, full):
    totals = lax.psum((jnp.sum(resid, axis=1), jnp.sum(resid * resid, axis=1)), "grp")
    centre = totals[0] / full
    spread = totals[1] / full - centre * centre
    inverse = lax.rsqrt(spread + NORM_EPSILON)
    normed = (resid - centre[:, None]) * inverse[:, None]
    return (normed * gain_row + bias_row, normed, inverse)


def normalize_back(out_grad, gain_row, normed, inverse, full):
    scaled = out_grad * gain_row
    totals = lax.psum((jnp.sum(scaled, axis=1), jnp.sum(scaled * normed, axis=1)), "grp")
    return inverse[:, None] * (
        scaled - totals[0][:, None] / full - normed * (totals[1][:, None] / full)
    )


def split_blocks(blocks, layer_index, groups):
    base = layer_index * (3 + 3 * groups)
    width = blocks.shape[1]
    w_query = blocks[base]
    w_key = blocks[base + 1]
    w_value = blocks[base + 2]
    w_out = blocks[base + 3 : base + 3 + groups].transpose(1, 0, 2).reshape(width, groups * width)
    w_up = (
        blocks[base + 3 + groups : base + 3 + 2 * groups]
        .transpose(1, 0, 2)
        .reshape(width, groups * width)
    )
    down_weight = blocks[base + 3 + 2 * groups : base + 3 + 3 * groups].reshape(
        groups * width, width
    )
    return (w_query, w_key, w_value, w_out, w_up, down_weight)


def masked_scores(queries, key_rows, segment_row):
    scale = queries.shape[2] ** (-0.5)
    scores = (
        jnp.einsum("qhd,khd->hqk", queries, key_rows, preferred_element_type=jnp.float32) * scale
    )
    allowed = segment_row[:, None] == segment_row[None, :]
    return jnp.where(allowed[None], scores, MASK_FILL)


def attend(item_set):
    queries, key_rows, value_rows, segment_row = item_set
    scores = masked_scores(queries, key_rows, segment_row)
    log_total = jax.nn.logsumexp(scores, axis=-1)
    probability = jnp.exp(scores - log_total[..., None])
    context = jnp.einsum(
        "hqk,khd->qhd",
        probability.astype(jnp.bfloat16),
        value_rows,
        preferred_element_type=jnp.float32,
    )
    return (context.astype(jnp.bfloat16), log_total)


def attend_back(item_set):
    queries, key_rows, value_rows, segment_row, log_total, context_grad = item_set
    scale = queries.shape[2] ** (-0.5)
    scores = masked_scores(queries, key_rows, segment_row)
    probability = jnp.exp(scores - log_total[..., None])
    value_grad = jnp.einsum(
        "hqk,qhd->khd",
        probability.astype(jnp.bfloat16),
        context_grad,
        preferred_element_type=jnp.float32,
    )
    prob_grad = jnp.einsum(
        "qhd,khd->hqk", context_grad, value_rows, preferred_element_type=jnp.float32
    )
    score_grad = probability * (
        prob_grad - jnp.sum(probability * prob_grad, axis=-1, keepdims=True)
    )
    score_low = score_grad.astype(jnp.bfloat16)
    query_grad = (
        jnp.einsum("hqk,khd->qhd", score_low, key_rows, preferred_element_type=jnp.float32) * scale
    )
    key_grad = (
        jnp.einsum("hqk,qhd->khd", score_low, queries, preferred_element_type=jnp.float32) * scale
    )
    return (query_grad, key_grad, value_grad)


def layer_forward(hidden, segments, blocks, vector_row_table, layer_index, groups):
    tokens_here, width = hidden.shape
    full = width * groups
    nup = vector_row_table.shape[0] - 8
    sequences, length = segments.shape
    per_group = HEADS // groups
    w_query, w_key, w_value, w_out, w_up, down_weight = split_blocks(blocks, layer_index, groups)
    x_low = hidden.astype(jnp.bfloat16)
    queries = (
        jnp.dot(x_low, w_query, preferred_element_type=jnp.float32) + vector_row_table[0]
    ).astype(jnp.bfloat16)
    key_rows = jnp.dot(x_low, w_key, preferred_element_type=jnp.float32).astype(jnp.bfloat16)
    value_rows = (
        jnp.dot(x_low, w_value, preferred_element_type=jnp.float32) + vector_row_table[1]
    ).astype(jnp.bfloat16)

    def heads(matrix):
        return matrix.reshape(sequences, length, per_group, width // per_group)

    context, log_total = lax.map(
        attend, (heads(queries), heads(key_rows), heads(value_rows), segments)
    )
    context = context.reshape(tokens_here, width)
    out_terms = jnp.dot(context, w_out, preferred_element_type=jnp.float32)
    mixed = lax.psum_scatter(out_terms, "grp", scatter_dimension=1, tiled=True)
    normed_in, normed_one, inverse_one = normalize(
        hidden + mixed + vector_row_table[2],
        vector_row_table[4 + nup],
        vector_row_table[5 + nup],
        full,
    )
    y_low = normed_in.astype(jnp.bfloat16)
    inner = jnp.dot(y_low, w_up, preferred_element_type=jnp.float32) + vector_row_table[
        3 : 3 + nup
    ].reshape(-1)
    gelu_output = exact_gelu(inner).astype(jnp.bfloat16)
    branch_output = (
        jnp.dot(gelu_output, down_weight, preferred_element_type=jnp.float32)
        + vector_row_table[3 + nup]
    )
    result, normed_two, inverse_two = normalize(
        normed_in + branch_output, vector_row_table[6 + nup], vector_row_table[7 + nup], full
    )
    saved = (
        x_low,
        queries,
        key_rows,
        value_rows,
        log_total,
        context,
        normed_one,
        inverse_one,
        y_low,
        inner,
        gelu_output,
        normed_two,
        inverse_two,
    )
    return (result, saved)


def layer_backward(out_grad, saved, segments, blocks, vector_row_table, layer_index, groups):
    (
        x_low,
        queries,
        key_rows,
        value_rows,
        log_total,
        context,
        normed_one,
        inverse_one,
        y_low,
        inner,
        gelu_output,
        normed_two,
        inverse_two,
    ) = saved
    tokens_here, width = out_grad.shape
    full = width * groups
    nup = vector_row_table.shape[0] - 8
    sequences, length = segments.shape
    per_group = HEADS // groups
    w_query, w_key, w_value, w_out, w_up, down_weight = split_blocks(blocks, layer_index, groups)

    def heads(matrix):
        return matrix.reshape(sequences, length, per_group, width // per_group)

    gain_two_grad = jnp.sum(out_grad * normed_two, axis=0)
    bias_two_grad = jnp.sum(out_grad, axis=0)
    second_grad = normalize_back(out_grad, vector_row_table[6 + nup], normed_two, inverse_two, full)
    down_bias_grad = jnp.sum(second_grad, axis=0)
    branch_low = second_grad.astype(jnp.bfloat16)
    down_grad = jnp.einsum("tf,tc->fc", gelu_output, branch_low, preferred_element_type=jnp.float32)
    act_grad = jnp.einsum("tc,fc->tf", branch_low, down_weight, preferred_element_type=jnp.float32)
    inner_grad = jax.vjp(exact_gelu, inner)[1](act_grad)[0]
    up_bias_grad = jnp.sum(inner_grad, axis=0)
    inner_low = inner_grad.astype(jnp.bfloat16)
    up_grad = jnp.einsum("tc,tf->cf", y_low, inner_low, preferred_element_type=jnp.float32)
    normed_grad = second_grad + jnp.einsum(
        "tf,cf->tc", inner_low, w_up, preferred_element_type=jnp.float32
    )
    gain_one_grad = jnp.sum(normed_grad * normed_one, axis=0)
    bias_one_grad = jnp.sum(normed_grad, axis=0)
    first_grad = normalize_back(
        normed_grad, vector_row_table[4 + nup], normed_one, inverse_one, full
    )
    out_bias_grad = jnp.sum(first_grad, axis=0)
    mixed_low = first_grad.astype(jnp.bfloat16)
    column_piece = lax.all_gather(mixed_low, "grp", axis=1, tiled=True)
    context_total = jnp.einsum("tn,cn->tc", column_piece, w_out, preferred_element_type=jnp.float32)
    weight_part = jnp.einsum("tc,tn->cn", context, column_piece, preferred_element_type=jnp.float32)
    context_low = context_total.astype(jnp.bfloat16)
    query_grad, key_grad, value_grad = lax.map(
        attend_back,
        (
            heads(queries),
            heads(key_rows),
            heads(value_rows),
            segments,
            log_total,
            heads(context_low),
        ),
    )
    query_grad = query_grad.reshape(tokens_here, width)
    key_grad = key_grad.reshape(tokens_here, width)
    value_grad = value_grad.reshape(tokens_here, width)
    query_bias_grad = jnp.sum(query_grad, axis=0)
    value_bias_grad = jnp.sum(value_grad, axis=0)
    query_low = query_grad.astype(jnp.bfloat16)
    key_low = key_grad.astype(jnp.bfloat16)
    value_low = value_grad.astype(jnp.bfloat16)
    w_query_grad = jnp.einsum("tc,td->cd", x_low, query_low, preferred_element_type=jnp.float32)
    w_key_grad = jnp.einsum("tc,td->cd", x_low, key_low, preferred_element_type=jnp.float32)
    w_value_grad = jnp.einsum("tc,td->cd", x_low, value_low, preferred_element_type=jnp.float32)
    in_grad = (
        first_grad
        + jnp.einsum("td,cd->tc", query_low, w_query, preferred_element_type=jnp.float32)
        + jnp.einsum("td,cd->tc", key_low, w_key, preferred_element_type=jnp.float32)
        + jnp.einsum("td,cd->tc", value_low, w_value, preferred_element_type=jnp.float32)
    )
    block_grads = jnp.concatenate(
        [
            w_query_grad[None],
            w_key_grad[None],
            w_value_grad[None],
            weight_part.reshape(width, groups, width).transpose(1, 0, 2),
            up_grad.reshape(width, groups, width).transpose(1, 0, 2),
            down_grad.reshape(groups, width, width),
        ],
        axis=0,
    )
    vector_grads = jnp.concatenate(
        [
            query_bias_grad[None],
            value_bias_grad[None],
            out_bias_grad[None],
            up_bias_grad.reshape(nup, width),
            down_bias_grad[None],
            gain_one_grad[None],
            bias_one_grad[None],
            gain_two_grad[None],
            bias_two_grad[None],
        ],
        axis=0,
    )
    return (in_grad, block_grads, vector_grads)


def adam_step(param, grad, first, second, decay, rate):
    first_new = BETA_ONE * first + (1.0 - BETA_ONE) * grad
    second_new = BETA_TWO * second + (1.0 - BETA_TWO) * grad * grad
    first_hat = first_new / (1.0 - BETA_ONE**STEP)
    second_hat = second_new / (1.0 - BETA_TWO**STEP)
    updated = param - rate * (first_hat / (jnp.sqrt(second_hat) + ADAM_EPSILON) + decay * param)
    return (updated, first_new, second_new)


def shards(
    tokens,
    segments,
    owners,
    masters,
    first_moment,
    second_moment,
    vectors,
    vector_first,
    vector_second,
    cotangent,
):
    groups = lax.axis_size("grp")
    capacity = masters.shape[1]
    width = tokens.shape[0]
    block_index, slot_of = slot_index(owners, groups, LAYERS, capacity)
    local_blocks = masters[0].reshape(capacity, width, width).astype(jnp.bfloat16)
    gathered = lax.all_gather(local_blocks, "row", axis=0, tiled=True)
    blocks = jnp.take(gathered, block_index, axis=0)
    hidden = tokens.astype(jnp.float32).T
    saved_layers = []
    for layer_index in range(LAYERS):
        hidden, saved = layer_forward(
            hidden, segments, blocks, vectors[layer_index], layer_index, groups
        )
        saved_layers.append(saved)
    flowing = cotangent.T
    block_parts = [None] * LAYERS
    vector_parts = [None] * LAYERS
    for layer_index in reversed(range(LAYERS)):
        flowing, block_parts[layer_index], vector_parts[layer_index] = layer_backward(
            flowing,
            saved_layers[layer_index],
            segments,
            blocks,
            vectors[layer_index],
            layer_index,
            groups,
        )
    block_grads = jnp.concatenate(block_parts, axis=0)
    vector_grads = jnp.stack(vector_parts, axis=0)
    flat_grads = block_grads.reshape(block_grads.shape[0], width * width)
    summed_blocks, summed_vectors = lax.psum((flat_grads, vector_grads), "row")
    own_row = lax.axis_index("row")
    targets = own_row * capacity + jnp.arange(capacity, dtype=jnp.int32)
    selector = (block_index[None, :] == targets[:, None]).astype(jnp.float32)
    own_grads = jnp.dot(selector, summed_blocks, precision=FULL_PRECISION)[None]
    new_masters, new_first, new_second = adam_step(
        masters, own_grads, first_moment, second_moment, WEIGHT_DECAY, LEARN_RATE
    )
    new_vectors, new_vector_first, new_vector_second = adam_step(
        vectors, summed_vectors, vector_first, vector_second, 0.0, VECTOR_RATE
    )
    return (
        hidden.T,
        flowing.T,
        new_masters,
        new_first,
        new_second,
        new_vectors,
        new_vector_first,
        new_vector_second,
    )


def solution(mesh):
    in_specs = (
        P("grp", "row"),
        P("row", None),
        P(),
        P("grp", "row", None),
        P("grp", "row", None),
        P("grp", "row", None),
        P(None, None, "grp"),
        P(None, None, "grp"),
        P(None, None, "grp"),
        P("grp", "row"),
    )
    out_specs = (
        P("grp", "row"),
        P("grp", "row"),
        P("grp", "row", None),
        P("grp", "row", None),
        P("grp", "row", None),
        P(None, None, "grp"),
        P(None, None, "grp"),
        P(None, None, "grp"),
    )
    return jax.shard_map(shards, mesh=mesh, in_specs=in_specs, out_specs=out_specs, check_vma=False)
```

profile of v0, /device:TPU:0, one launch (start us, length us, event | category | flops | bytes accessed | tf_op | source)
XLA Modules:
  0.0 1041.6 jit_solution(12224619097191868718)
XLA Ops:
  12.0 66.1 %all-gather.4.cloned.1.call-done = bf16[64,192,192]{2,1,0:T(8,128)(2,1)} async-done(((bf16[8,192,192]{2,1,0:T(8,128)(2,1)}), bf16[64,192,192]{2,1,0:T(8,128)(2,1)}) %all-gather.4.cloned.1.call-update) | async-done | bytes 4718608 | tf_op jit(solution)/shard_map/all_gather | solution.py:340
  97.3 25.4 %while.52 = (s32[]{:T(128)}, bf16[5,512,3,64]{1,3,2,0:T(8,128)(2,1)}, f32[5,3,512]{2,1,0:T(4,128)S(1)}, bf16[5,512,3,64]{1,3,2,0:T(8,128)(2,1)}, s32[5,512]{1,0:...) while((s32[]{:T(128)}, ...), condition=%wide.region_5.6_spmd, body=%wide.region_2.0_spmd.sunk | while | flops 210350080 | bytes 11360349 | solution.py:165
  130.1 5.6 fusion.184
  139.5 78.5 %reduce-scatter.3.cloned.1.call-done = f32[2560,192]{0,1:T(8,128)} async-done(((f32[2560,768]{0,1:T(8,128)}), f32[2560,192]{0,1:T(8,128)}) %reduce-scatter.3.cloned.1.call-update) | async-done | bytes 1966096 | tf_op jit(solution)/shard_map/reduce_scatter | solution.py:170
  220.6 15.8 %all-reduce.7 = (f32[2560]{0:T(1024)S(1)}, f32[2560]{0:T(1024)S(1)}) all-reduce(f32[2560]{0:T(1024)} %get-tuple-element.426, f32[2560]{0:T(1024)S(1)} %get-tuple-element.425), channel_id=1, replica_groups=mesh['grp'=4,'row'=8] {'grp'}, use_global_device_ids=true, to_apply=%region_10.11 | all-reduce | flops 5120 | bytes 40960 | tf_op jit(solution)/shard_map/psum | solution.py:62
  236.4 20.7 %multiply_convert_fusion.3 = (bf16[2560,768]{1,0:T(8,128)(2,1)S(1)}, f32[2560,768]{1,0:T(8,128)}, f32[2560,768]{1,0:T(8,128)}) fusion(f32[768]{0:T(1024)} %add.341, bf16[192,768]{1,0:T(8,128)(2,1)S(1)} %reshape.429, f32[2560,192]{0,1:T(8,128)S(1)} %get-tuple-element.532, f32[192]{0:T(256)} %bitcast.527, f32[192]{0:T(256)} %bitcast.494, ...), kind=kOutput, calls=%fused_computation.148 | convolution fusion | flops 887193600 | bytes 21946880 | tf_op jit(solution)/shard_map/dot_general | solution.py:178
  257.2 4.7 fusion.163
  261.9 15.6 %all-reduce.6 = (f32[2560]{0:T(1024)S(1)}, f32[2560]{0:T(1024)S(1)}) all-reduce(f32[2560]{0:T(1024)S(1)} %get-tuple-element.424, f32[2560]{0:T(1024)S(1)} %get-tuple-element.423), channel_id=1, replica_groups=mesh['grp'=4,'row'=8] {'grp'}, use_global_device_ids=true, to_apply=%region_14.15 | all-reduce | flops 5120 | bytes 40960 | tf_op jit(solution)/shard_map/psum | solution.py:62
  304.8 30.0 %while.53 = (s32[]{:T(128)}, bf16[5,512,3,64]{1,3,2,0:T(8,128)(2,1)}, f32[5,3,512]{2,1,0:T(4,128)S(1)}, bf16[5,512,3,64]{1,3,2,0:T(8,128)(2,1)}, s32[5,512]{1,0:...) while((s32[]{:T(128)}, ...), condition=%wide.region_18.19_spmd, body=%wide.region_15.18_spmd.sunk | while | flops 210350080 | bytes 11360349 | solution.py:165
  338.2 4.3 fusion.185
  347.3 78.8 %reduce-scatter.5.cloned.1.call-done = f32[2560,192]{0,1:T(8,128)} async-done(((f32[2560,768]{0,1:T(8,128)}), f32[2560,192]{0,1:T(8,128)}) %reduce-scatter.5.cloned.1.call-update) | async-done | bytes 1966096 | tf_op jit(solution)/shard_map/reduce_scatter | solution.py:170
  426.1 4.3 fusion.162
  430.4 16.8 %all-reduce.5 = (f32[2560]{0:T(1024)}, f32[2560]{0:T(1024)}) all-reduce(f32[2560]{0:T(1024)} %get-tuple-element.422, f32[2560]{0:T(1024)} %get-tuple-element.421), channel_id=1, replica_groups=mesh['grp'=4,'row'=8] {'grp'}, use_global_device_ids=true, to_apply=%region_23.24 | all-reduce | flops 5120 | bytes 40960 | tf_op jit(solution)/shard_map/psum | solution.py:62
  447.9 21.2 %multiply_convert_fusion.2 = (bf16[2560,768]{1,0:T(8,128)(2,1)S(1)}, f32[2560,768]{1,0:T(8,128)}, f32[2560,768]{1,0:T(8,128)}) fusion(f32[768]{0:T(1024)} %add.366, bf16[192,768]{1,0:T(8,128)(2,1)S(1)} %reshape.436, f32[2560,192]{0,1:T(8,128)} %get-tuple-element.529, f32[192]{0:T(256)} %bitcast.530, f32[192]{0:T(256)} %bitcast.499, ...), kind=kOutput, calls=%fused_computation.135 | convolution fusion | flops 887193600 | bytes 21946880 | tf_op jit(solution)/shard_map/dot_general | solution.py:178
  472.8 16.2 %all-reduce.4 = (f32[2560]{0:T(1024)}, f32[2560]{0:T(1024)}) all-reduce(f32[2560]{0:T(1024)} %get-tuple-element.420, f32[2560]{0:T(1024)} %get-tuple-element.419), channel_id=1, replica_groups=mesh['grp'=4,'row'=8] {'grp'}, use_global_device_ids=true, to_apply=%region_27.28 | all-reduce | flops 5120 | bytes 40960 | tf_op jit(solution)/shard_map/psum | solution.py:62
  494.3 16.4 %all-reduce.3 = (f32[2560]{0:T(1024)}, f32[2560]{0:T(1024)}) all-reduce(f32[2560]{0:T(1024)} %get-tuple-element.409, f32[2560]{0:T(1024)} %get-tuple-element.413), channel_id=1, replica_groups=mesh['grp'=4,'row'=8] {'grp'}, use_global_device_ids=true, to_apply=%region_31.32 | all-reduce | flops 5120 | bytes 40960 | tf_op jit(solution)/shard_map/psum | solution.py:72
  512.1 4.9 fusion.169
  517.1 9.1 fusion.182
  529.7 15.3 %all-reduce.2 = (f32[2560]{0:T(1024)S(1)}, f32[2560]{0:T(1024)S(1)}) all-reduce(f32[2560]{0:T(1024)} %get-tuple-element.411, f32[2560]{0:T(1024)} %get-tuple-element.412), channel_id=1, replica_groups=mesh['grp'=4,'row'=8] {'grp'}, use_global_device_ids=true, to_apply=%region_35.36 | all-reduce | flops 5120 | bytes 40960 | tf_op jit(solution)/shard_map/psum | solution.py:72
  552.9 48.7 %all-gather.6.cloned.1.call-done = bf16[2560,768]{0,1:T(8,128)(2,1)} async-done(((bf16[2560,192]{0,1:T(8,128)(2,1)}), bf16[2560,768]{0,1:T(8,128)(2,1)}) %all-gather.6.cloned.1.call-update) | async-done | bytes 3932176 | tf_op jit(solution)/shard_map/all_gather | solution.py:254
  615.0 59.3 %while.54 = (s32[]{:T(128)}, f32[5,512,3,64]{1,3,2,0:T(8,128)}, bf16[5,512,3,64]{1,3,2,0:T(8,128)(2,1)}, f32[5,512,3,64]{1,3,2,0:T(8,128)}, bf16[5,512,3,64]{1,3...) while((s32[]{:T(128)}, f32[5,512,3,64]{1,3,2,0:T(8,128)}, ...), condition=%wide.region_38.39_spmd, body=%wide.region_36.38_spmd.sunk | while | flops 510851584 | bytes 26717300 | solution.py:258
  690.8 15.8 %all-reduce.1 = (f32[2560]{0:T(1024)S(1)}, f32[2560]{0:T(1024)S(1)}) all-reduce(f32[2560]{0:T(1024)S(1)} %get-tuple-element.405, f32[2560]{0:T(1024)S(1)} %get-tuple-element.415), channel_id=1, replica_groups=mesh['grp'=4,'row'=8] {'grp'}, use_global_device_ids=true, to_apply=%region_42.43 | all-reduce | flops 5120 | bytes 40960 | tf_op jit(solution)/shard_map/psum | solution.py:72
  709.6 9.1 fusion.183
  722.2 15.1 %all-reduce = (f32[2560]{0:T(1024)S(1)}, f32[2560]{0:T(1024)S(1)}) all-reduce(f32[2560]{0:T(1024)S(1)} %get-tuple-element.407, f32[2560]{0:T(1024)S(1)} %get-tuple-element.414), channel_id=1, replica_groups=mesh['grp'=4,'row'=8] {'grp'}, use_global_device_ids=true, to_apply=%region_46.47 | all-reduce | flops 5120 | bytes 40960 | tf_op jit(solution)/shard_map/psum | solution.py:72
  748.2 4.6 fusion.143
  753.3 4.5 fusion.131
  777.6 4.9 fusion.140
  803.2 55.8 %while.55 = (s32[]{:T(128)}, f32[5,512,3,64]{1,3,2,0:T(8,128)S(1)}, bf16[5,512,3,64]{1,3,2,0:T(8,128)(2,1)}, f32[5,512,3,64]{1,3,2,0:T(8,128)}, bf16[5,512,3,64]...) while((s32[]{:T(128)}, f32[5,512,3,64]{1,3,2,0:T(8,128)S(1)}, ...), condition=%wide.region_49.50_spmd, body=%wide.region_47.49_spmd.sunk | while | flops 510851584 | bytes 26715252 | solution.py:258
  882.7 38.4 %concatenate.46 = f32[30,36864]{1,0:T(8,128)} concatenate(f32[1,36864]{1,0:T(1,128)} %concatenate.34, f32[1,36864]{1,0:T(1,128)S(1)} %concatenate.35, f32[1,36864]{1,0:T(1,128)} %concatenate.36, f32[4,36864]{1,0:T(4,128)} %concatenate.37, f32[4,36864]{1,0:T(4,128)} %concatenate.38, f32[4,36864]{1,0:T(4,128)} %concatenate.39, f32[1,36864]{1,0:T(1,128)} %concatenate.40, ...), dimensions={0} | concatenate | bytes 8847360 | tf_op jit(solution)/shard_map/concatenate | solution.py:362
  923.5 27.7 %psum.143 = f32[2,12,192]{2,1,0:T(8,128)S(1)} all-reduce(f32[2,12,192]{2,1,0:T(8,128)S(1)} %pad_maximum_fusion), channel_id=1, replica_groups=mesh['grp'=4,'row'=8] {'row'}, use_global_device_ids=true, to_apply=%region_69.70 | all-reduce | flops 4608 | bytes 36864 | tf_op jit(solution)/shard_map/psum | solution.py:365
  959.4 68.4 %all-reduce.10.cloned.1.call-done = f32[30,36864]{1,0:T(8,128)} async-done(((f32[30,36864]{1,0:T(8,128)}), f32[30,36864]{1,0:T(8,128)}) %all-reduce.10.cloned.1.call-update) | async-done | bytes 4423696 | tf_op jit(solution)/shard_map/psum | solution.py:365
  1027.8 6.5 multiply_subtract_fusion
  (547 shorter events, 386.7 us)
Async XLA Ops:
  7.2 70.8 %all-gather.4.cloned.1.call-start = ((), (), s32[]{:S(2)}) async-start(), calls=%async_computation.2 | async-start | bytes 7077888 | tf_op jit(solution)/shard_map/all_gather | solution.py:340
  10.4 207.5 %reduce-scatter.3.cloned.1.call-start = ((), (), s32[]{:S(2)}) async-start(), calls=%async_computation.3 | async-start | bytes 9830400 | tf_op jit(solution)/shard_map/reduce_scatter | solution.py:170
  135.8 290.3 %reduce-scatter.5.cloned.1.call-start = ((), (), s32[]{:S(2)}) async-start(), calls=%async_computation.4 | async-start | bytes 9830400 | tf_op jit(solution)/shard_map/reduce_scatter | solution.py:170
  138.8 97.6 %copy-start.41 = (bf16[192,768]{1,0:T(8,128)(2,1)}, bf16[192,768]{1,0:T(8,128)(2,1)S(1)}, u32[]{:S(2)}) copy-start(bf16[192,768]{1,0:T(8,128)(2,1)S(1)} %reshape.429) | copy-start | bytes 884740
  220.6 36.6 %copy-start.4 = (f32[2560,192]{0,1:T(8,128)}, f32[2560,192]{0,1:T(8,128)S(1)}, u32[]{:S(2)}) copy-start(f32[2560,192]{0,1:T(8,128)S(1)} %get-tuple-element.532) | copy-start | bytes 5898244
  236.4 20.8 %copy-start.52 = (f32[2560]{0:T(1024)}, f32[2560]{0:T(1024)S(1)}, u32[]{:S(2)}) copy-start(f32[2560]{0:T(1024)S(1)} %get-tuple-element.582) | copy-start | bytes 30724
  236.4 20.8 %copy-start.54 = (f32[2560]{0:T(1024)}, f32[2560]{0:T(1024)S(1)}, u32[]{:S(2)}) copy-start(f32[2560]{0:T(1024)S(1)} %get-tuple-element.583) | copy-start | bytes 30724
  236.4 20.8 %copy-start.44 = (bf16[4,192,192]{2,1,0:T(8,128)(2,1)S(1)}, bf16[4,192,192]{2,1,0:T(8,128)(2,1)}, u32[]{:S(2)}) copy-start(bf16[4,192,192]{2,1,0:T(8,128)(2,1)} %get-tuple-element.546) | copy-start | bytes 884740
  236.4 20.8 %copy-start.69 = (f32[1,1,192]{2,0,1:T(1,128)S(1)}, f32[1,1,192]{2,0,1:T(1,128)}, u32[]{:S(2)}) copy-start(f32[1,1,192]{2,0,1:T(1,128)} %get-tuple-element.571) | copy-start | bytes 2308
  236.4 20.8 %copy-start.97 = (f32[1,1,192]{2,0,1:T(1,128)S(1)}, f32[1,1,192]{2,0,1:T(1,128)}, u32[]{:S(2)}) copy-start(f32[1,1,192]{2,0,1:T(1,128)} %get-tuple-element.570) | copy-start | bytes 2308
  236.4 20.8 %copy-start.101 = (f32[1,1,192]{2,0,1:T(1,128)S(1)}, f32[1,1,192]{2,0,1:T(1,128)}, u32[]{:S(2)}) copy-start(f32[1,1,192]{2,0,1:T(1,128)} %get-tuple-element.569) | copy-start | bytes 2308
  257.2 20.3 %copy-start.74 = (f32[1,1,192]{2,0,1:T(1,128)S(1)}, f32[1,1,192]{2,0,1:T(1,128)}, u32[]{:S(2)}) copy-start(f32[1,1,192]{2,0,1:T(1,128)} %get-tuple-element.567) | copy-start | bytes 2308
  277.9 17.2 %copy-start.2 = (bf16[2560,192]{0,1:T(8,128)(2,1)}, bf16[2560,192]{0,1:T(8,128)(2,1)S(1)}, u32[]{:S(2)}) copy-start(bf16[2560,192]{0,1:T(8,128)(2,1)S(1)} %fusion.135) | copy-start | bytes 2949124
  342.6 259.0 %all-gather.6.cloned.1.call-start = ((), (), s32[]{:S(2)}) async-start(), calls=%async_computation.5 | async-start | bytes 4915200 | tf_op jit(solution)/shard_map/all_gather | solution.py:254
  447.9 21.3 %copy-start.56 = (f32[2560]{0:T(1024)}, f32[2560]{0:T(1024)S(1)}, u32[]{:S(2)}) copy-start(f32[2560]{0:T(1024)S(1)} %get-tuple-element.578) | copy-start | bytes 30724
  447.9 21.3 %copy-start.59 = (f32[2560]{0:T(1024)}, f32[2560]{0:T(1024)S(1)}, u32[]{:S(2)}) copy-start(f32[2560]{0:T(1024)S(1)} %get-tuple-element.579) | copy-start | bytes 30724
  447.9 21.3 %copy-start.6 = (f32[2560,192]{0,1:T(8,128)S(1)}, f32[2560,192]{0,1:T(8,128)}, u32[]{:S(2)}) copy-start(f32[2560,192]{0,1:T(8,128)} %get-tuple-element.529) | copy-start | bytes 5898244
  447.9 21.3 %copy-start.46 = (bf16[4,192,192]{2,1,0:T(8,128)(2,1)S(1)}, bf16[4,192,192]{2,1,0:T(8,128)(2,1)}, u32[]{:S(2)}) copy-start(bf16[4,192,192]{2,1,0:T(8,128)(2,1)} %get-tuple-element.543) | copy-start | bytes 884740
  447.9 21.3 %copy-start.71 = (f32[1,1,192]{2,0,1:T(1,128)S(1)}, f32[1,1,192]{2,0,1:T(1,128)}, u32[]{:S(2)}) copy-start(f32[1,1,192]{2,0,1:T(1,128)} %get-tuple-element.563) | copy-start | bytes 2308
  447.9 21.3 %copy-start.98 = (f32[1,1,192]{2,0,1:T(1,128)S(1)}, f32[1,1,192]{2,0,1:T(1,128)}, u32[]{:S(2)}) copy-start(f32[1,1,192]{2,0,1:T(1,128)} %get-tuple-element.562) | copy-start | bytes 2308
  447.9 21.3 %copy-start.100 = (f32[1,1,192]{2,0,1:T(1,128)S(1)}, f32[1,1,192]{2,0,1:T(1,128)}, u32[]{:S(2)}) copy-start(f32[1,1,192]{2,0,1:T(1,128)} %get-tuple-element.561) | copy-start | bytes 2308
  550.8 245.9 %all-gather.8.cloned.1.call-start = ((), (), s32[]{:S(2)}) async-start(), calls=%async_computation.6 | async-start | bytes 4915200 | tf_op jit(solution)/shard_map/all_gather | solution.py:254
  709.5 9.2 copy-start.20
  742.4 285.4 %all-reduce.10.cloned.1.call-start = ((), (), s32[]{:S(2)}) async-start(), calls=%async_computation.7 | async-start | bytes 9437184 | tf_op jit(solution)/shard_map/psum | solution.py:365
  921.2 30.0 %copy-start.65 = (f32[2,12,192]{2,0,1:T(2,128)S(1)}, f32[2,12,192]{2,0,1:T(2,128)}, u32[]{:S(2)}) copy-start(f32[2,12,192]{2,0,1:T(2,128)} %param.27) | copy-start | bytes 55300
  921.2 30.0 %copy-start.66 = (f32[2,12,192]{2,0,1:T(2,128)S(1)}, f32[2,12,192]{2,0,1:T(2,128)}, u32[]{:S(2)}) copy-start(f32[2,12,192]{2,0,1:T(2,128)} %param.28) | copy-start | bytes 55300
  921.3 30.0 %copy-start.67 = (f32[2,12,192]{2,0,1:T(2,128)S(1)}, f32[2,12,192]{2,0,1:T(2,128)}, u32[]{:S(2)}) copy-start(f32[2,12,192]{2,0,1:T(2,128)} %param.29) | copy-start | bytes 55300
  922.8 32.4 %copy-start.28 = (bf16[24,8,5,512]{3,1,2,0:T(8,128)(2,1)S(1)}, bf16[24,8,5,512]{3,1,2,0:T(8,128)(2,1)}, u32[]{:S(2)}) copy-start(bf16[24,8,5,512]{3,1,2,0:T(8,128)(2,1)} %copy-done.27) | copy-start | bytes 2949124
  956.6 71.2 %copy-start.31 = (f32[1,8,36864]{2,1,0:T(8,128)S(1)}, f32[1,8,36864]{2,1,0:T(8,128)}, u32[]{:S(2)}) copy-start(f32[1,8,36864]{2,1,0:T(8,128)} %param.24) | copy-start | bytes 3538948
  956.6 71.2 %copy-start.39 = (f32[1,8,36864]{2,1,0:T(8,128)S(1)}, f32[1,8,36864]{2,1,0:T(8,128)}, u32[]{:S(2)}) copy-start(f32[1,8,36864]{2,1,0:T(8,128)} %param.25) | copy-start | bytes 3538948
  956.7 71.2 %copy-start.40 = (f32[1,8,36864]{2,1,0:T(8,128)S(1)}, f32[1,8,36864]{2,1,0:T(8,128)}, u32[]{:S(2)}) copy-start(f32[1,8,36864]{2,1,0:T(8,128)} %param.26) | copy-start | bytes 3538948
  956.7 71.1 %copy-start.95 = (s32[30]{0:T(128)S(1)}, s32[30]{0:T(128)}, u32[]{:S(2)}) copy-start(s32[30]{0:T(128)} %copy-done.94) | copy-start | bytes 364
  (81 other events, 329.1 us)
Sparse Core Ops, SparseCore 0:
  10.5 67.4 all-gather.3
  135.9 81.9 reduce-scatter.2
  342.7 83.3 reduce-scatter.4
  551.0 50.5 all-gather.5
  742.5 50.5 all-gather.7
  921.4 106.3 all-reduce.9
where the time goes:
time: 1060 us; the launch traced here: 1040 us
  waiting for transfers between devices  341 us (32%)
  matrix products  285 us (27%)
  local copies, waits for them, and re-layouts  182 us (17%)
  blocking collectives  155 us (15%)
  other arithmetic  62.1 us (6%)
  between operations  15.9 us (2%)
    reduce_scatter x2, waiting for transfers between devices, layer_forward(): mixed = lax.psum_scatter(out_terms, 'grp', scatter_dimension=1, tiled=True)  157 us
    psum x1, waiting for transfers between devices, shards(): summed_blocks, summed_vectors = lax.psum((flat_grads, vector_grads), 'row')  68.4 us
    all_gather x1, waiting for transfers between devices, shards(): gathered = lax.all_gather(local_blocks, 'row', axis=0, tiled=True)  66.1 us
    psum x4, blocking collectives, normalize(): lax.psum((jnp.sum(resid, axis=1), jnp.sum(resid * resid, axis=1)), 'grp')  64.4 us
    psum x4, blocking collectives, normalize_back(): lax.psum((jnp.sum(scaled, axis=1), jnp.sum(scaled * normed, axis=1)), 'grp')  62.6 us
    concatenate x13, local copies, waits for them, and re-layouts, shards(): block_grads = jnp.concatenate(block_parts, axis=0)  57.7 us
    all_gather x2, waiting for transfers between devices, layer_backward(): column_piece = lax.all_gather(mixed_low, 'grp', axis=1, tiled=True)  48.7 us
    dot_general x2, matrix products, layer_forward(): jnp.dot(y_low, w_up, preferred_element_type=jnp.float32)  42 us
  transfers between devices with their start and end apart: 6, of which 5 were waited for; matrix products, arithmetic and copies ran while one was open for 7% of the time, Pallas kernels for 0%

commit v1 on v0

v1 whole, which is shorter than its diff:
```python
import functools
import math

import jax
import jax.numpy as jnp
import numpy as np
from jax import lax
from jax.experimental import pallas as pl
from jax.experimental.pallas import tpu as pltpu
from jax.sharding import PartitionSpec as P

HEADS = 12
LAYERS = 2
STEP = 7
BETA_ONE = 0.9
BETA_TWO = 0.999
LEARN_RATE = 0.1
VECTOR_RATE = 0.5
WEIGHT_DECAY = 0.01
ADAM_EPSILON = 1e-08
NORM_EPSILON = 1e-12
MASK_FILL = -1e30
AUG = 16
LANES = 128
VMEM_LIMIT = 48 * 1024 * 1024
F32 = jnp.float32
BF16 = jnp.bfloat16


def nn(a, b):
    return lax.dot_general(a, b, (((1,), (0,)), ((), ())), preferred_element_type=F32)


def nt(a, b):
    return lax.dot_general(a, b, (((1,), (1,)), ((), ())), preferred_element_type=F32)


def tn(a, b):
    return lax.dot_general(a, b, (((0,), (0,)), ((), ())), preferred_element_type=F32)


def block_layout(groups, layers):
    counts = []
    block_matrix = []
    block_step = []
    for layer_index in range(layers):
        for matrix_type in range(6):
            amount = 1 if matrix_type < 3 else groups
            for position in range(amount):
                block_matrix.append(layer_index * 6 + matrix_type)
                block_step.append(position)
            counts.append(amount)
    return (
        np.array(counts, np.int32),
        np.array(block_matrix, np.int32),
        np.array(block_step, np.int32),
    )


def slot_index(owners, groups, layers, capacity):
    counts, block_matrix, block_step = block_layout(groups, layers)
    matrix_ids = jnp.arange(counts.shape[0], dtype=jnp.int32)
    same_owner = owners[:, None] == owners[None, :]
    earlier = matrix_ids[None, :] < matrix_ids[:, None]
    slot_of = jnp.sum(
        jnp.where(same_owner & earlier, jnp.asarray(counts, jnp.int32)[None, :], 0), axis=1
    )
    starts = owners * capacity + slot_of
    choose = (jnp.asarray(block_matrix, jnp.int32)[:, None] == matrix_ids[None, :]).astype(
        jnp.int32
    )
    return jnp.sum(choose * starts[None, :], axis=1) + jnp.asarray(block_step, jnp.int32)


def lanes(value):
    total = value[:, :LANES]
    for at in range(LANES, value.shape[1], LANES):
        total = total + value[:, at : at + LANES]
    return total


def first_step():
    return pl.program_id(0) == 0


def accumulate(ref, index, value):
    @pl.when(first_step())
    def _():
        ref[index] = value

    @pl.when(jnp.logical_not(first_step()))
    def _():
        ref[index] = ref[index] + value


def col_sums(a, b):
    return jnp.concatenate(
        [jnp.sum(a, axis=0, keepdims=True), jnp.sum(b, axis=0, keepdims=True)], axis=0
    )


def gathered(stats):
    return (stats[0][...] + stats[1][...]) + (stats[2][...] + stats[3][...])


def moments(stats, full):
    total = gathered(stats)
    centre = total[0:1] * (1.0 / full)
    spread = total[1:2] * (1.0 / full) - centre * centre
    return centre, lax.rsqrt(jnp.maximum(spread, 0.0) + NORM_EPSILON)


def split3(value):
    high = value.astype(BF16)
    rest = value - high.astype(F32)
    mid = rest.astype(BF16)
    last = (rest - mid.astype(F32)).astype(BF16)
    return high, mid, last


def segment_rows(segs):
    row = lax.broadcasted_iota(jnp.int32, (AUG, segs.shape[1]), 0)
    same = row == segs
    query_rows = jnp.where(same | (row >= 4), 0.0, MASK_FILL)
    key_rows = jnp.where(same | ((row >= 4) & (row < 7)), 1.0, 0.0)
    return query_rows, key_rows.astype(BF16)


def with_rows(query_rows, value):
    high, mid, last = split3(-value)
    row = lax.broadcasted_iota(jnp.int32, query_rows.shape, 0)
    out = jnp.where(row == 4, high.astype(F32), query_rows)
    out = jnp.where(row == 5, mid.astype(F32), out)
    out = jnp.where(row == 6, last.astype(F32), out)
    return out.astype(BF16)


def norm_cdf(u):
    a = jnp.abs(u) * math.sqrt(0.5)
    t = 1.0 / (1.0 + 0.3275911 * a)
    bell = jnp.exp(-a * a)
    poly = t * (
        0.254829592
        + t * (-0.284496736 + t * (1.421413741 + t * (-1.453152027 + t * 1.061405429)))
    )
    tail = (0.5 * poly) * bell
    return jnp.where(u < 0, tail, 1.0 - tail), bell * (1.0 / math.sqrt(2.0 * math.pi))


def attend_body(first, per_group, full, *refs):
    refs = list(refs)
    if first:
        x_ref = refs.pop(0)
    else:
        r2_ref = refs.pop(0)
        stats = [refs.pop(0) for _ in range(4)]
        prev_ref = refs.pop(0)
    seg_ref, w_ref, vec_ref = refs[:3]
    refs = refs[3:]
    if not first:
        x2_ref, mi_ref = refs[:2]
        refs = refs[2:]
    qkv_ref, low_ref, high_ref, lse_ref = refs[:4]
    width = w_ref.shape[1]
    size = width // per_group
    vec = vec_ref[...]
    if first:
        x = x_ref[...]
    else:
        centre, inverse = moments(stats, full)
        prev = prev_ref[...]
        nup = prev.shape[1] - 8
        x2 = (r2_ref[...] - centre) * inverse * prev[:, 6 + nup : 7 + nup] + prev[
            :, 7 + nup : 8 + nup
        ]
        x2_ref[...] = x2
        mi_ref[...] = jnp.concatenate([centre, inverse], axis=0)
        x = x2.astype(BF16)
    q = (tn(w_ref[0], x) + vec[:, 0:1]).astype(BF16)
    k = tn(w_ref[1], x).astype(BF16)
    v = (tn(w_ref[2], x) + vec[:, 1:2]).astype(BF16)
    qkv_ref[0:width] = q
    qkv_ref[width : 2 * width] = k
    qkv_ref[2 * width : 3 * width] = v
    query_rows, key_rows = segment_rows(seg_ref[0])
    query_rows = query_rows.astype(BF16)
    scale = size ** (-0.5)
    length = x.shape[1]
    tile = 256
    for h in range(per_group):
        part = slice(h * size, (h + 1) * size)
        qa = jnp.concatenate([q[part] * jnp.asarray(scale, BF16), query_rows], axis=0)
        ka = jnp.concatenate([k[part], key_rows], axis=0)
        for at in range(0, length, tile):
            cols = slice(at, at + tile)
            s = tn(ka, qa[:, cols])
            top = jnp.max(s, axis=0, keepdims=True)
            e = jnp.exp(s - top)
            total = jnp.sum(e, axis=0, keepdims=True)
            ctx = (nn(v[part], e.astype(BF16)) * (1.0 / total)).astype(BF16)
            lse_ref[h : h + 1, cols] = top + jnp.log(total)
            half = width // 2
            lo, hi = h * size, (h + 1) * size
            if hi <= half:
                low_ref[lo:hi, cols] = ctx
            elif lo >= half:
                high_ref[lo - half : hi - half, cols] = ctx
            else:
                low_ref[lo:half, cols] = ctx[: half - lo]
                high_ref[0 : hi - half, cols] = ctx[half - lo :]


def out_body(x_ref, *refs):
    pieces = refs[:8]
    w_ref, vec_ref, r1_ref, st_ref = refs[8:]
    groups = w_ref.shape[0]
    total = x_ref[...].astype(F32) + vec_ref[...][:, 2:3]
    for g in range(groups):
        piece = jnp.concatenate([pieces[2 * g][...], pieces[2 * g + 1][...]], axis=0)
        total = total + tn(w_ref[g], piece)
    r1_ref[...] = total
    st_ref[...] = col_sums(total, total * total)


def mlp_body(full, r1_ref, s0, s1, s2, s3, wu_ref, wd_ref, vec_ref, r2_ref, mi_ref, hid_ref, gp_ref, st_ref):
    groups = wu_ref.shape[0]
    width = r1_ref.shape[0]
    vec = vec_ref[...]
    nup = vec.shape[1] - 8
    centre, inverse = moments((s0, s1, s2, s3), full)
    mi_ref[...] = jnp.concatenate([centre, inverse], axis=0)
    y1 = (r1_ref[...] - centre) * inverse * vec[:, 4 + nup : 5 + nup] + vec[:, 5 + nup : 6 + nup]
    yl = y1.astype(BF16)
    total = y1 + vec[:, 3 + nup : 4 + nup]
    for j in range(groups):
        u = tn(wu_ref[j], yl) + vec[:, 3 + j : 4 + j]
        cdf, bell = norm_cdf(u)
        hid = (u * cdf).astype(BF16)
        hid_ref[j * width : (j + 1) * width] = hid
        gp_ref[j * width : (j + 1) * width] = (cdf + u * bell).astype(BF16)
        total = total + tn(wd_ref[j], hid)
    r2_ref[...] = total
    st_ref[...] = col_sums(total, total * total)


def last_body(full, r2_ref, s0, s1, s2, s3, cot_ref, vec_ref, _, out_ref, mi_ref, st_ref, acc_ref):
    vec = vec_ref[...]
    nup = vec.shape[1] - 8
    centre, inverse = moments((s0, s1, s2, s3), full)
    mi_ref[...] = jnp.concatenate([centre, inverse], axis=0)
    n2 = (r2_ref[...] - centre) * inverse
    gain = vec[:, 6 + nup : 7 + nup]
    out_ref[...] = n2 * gain + vec[:, 7 + nup : 8 + nup]
    dy = cot_ref[...]
    e = dy * gain
    st_ref[...] = col_sums(e, e * n2)
    accumulate(acc_ref, 0, lanes(dy * n2))
    accumulate(acc_ref, 1, lanes(dy))


def mlp_back_body(
    full, dy_ref, r2_ref, mi2_ref, s0, s1, s2, s3, r1_ref, mi1_ref, hid_ref, gp_ref, wu_ref, wd_ref, vec_ref,
    dy1_ref, st_ref, gup_ref, gdown_ref, acc_ref,
):
    groups = wu_ref.shape[0]
    width = r1_ref.shape[0]
    vec = vec_ref[...]
    nup = vec.shape[1] - 8
    sums = gathered((s0, s1, s2, s3)) * (1.0 / full)
    mi2 = mi2_ref[...]
    n2 = (r2_ref[...] - mi2[0:1]) * mi2[1:2]
    e = dy_ref[...] * vec[:, 6 + nup : 7 + nup]
    dz = mi2[1:2] * (e - sums[0:1] - n2 * sums[1:2])
    accumulate(acc_ref, groups, lanes(dz))
    dzl = dz.astype(BF16)
    mi1 = mi1_ref[...]
    n1 = (r1_ref[...] - mi1[0:1]) * mi1[1:2]
    gain1 = vec[:, 4 + nup : 5 + nup]
    yl = (n1 * gain1 + vec[:, 5 + nup : 6 + nup]).astype(BF16)
    dy1 = dz
    for j in range(groups):
        rows = slice(j * width, (j + 1) * width)
        accumulate(gdown_ref, j, nt(hid_ref[rows], dzl))
        du = nn(wd_ref[j], dzl) * gp_ref[rows].astype(F32)
        accumulate(acc_ref, j, lanes(du))
        dul = du.astype(BF16)
        accumulate(gup_ref, j, nt(yl, dul))
        dy1 = dy1 + nn(wu_ref[j], dul)
    dy1_ref[...] = dy1
    e1 = dy1 * gain1
    st_ref[...] = col_sums(e1, e1 * n1)
    accumulate(acc_ref, groups + 1, lanes(dy1 * n1))
    accumulate(acc_ref, groups + 2, lanes(dy1))


def norm_back_body(full, dy1_ref, r1_ref, mi1_ref, s0, s1, s2, s3, vec_ref, dr1_ref, low_ref, high_ref, acc_ref):
    vec = vec_ref[...]
    nup = vec.shape[1] - 8
    sums = gathered((s0, s1, s2, s3)) * (1.0 / full)
    mi1 = mi1_ref[...]
    n1 = (r1_ref[...] - mi1[0:1]) * mi1[1:2]
    e = dy1_ref[...] * vec[:, 4 + nup : 5 + nup]
    dr = mi1[1:2] * (e - sums[0:1] - n1 * sums[1:2])
    dr1_ref[...] = dr
    accumulate(acc_ref, 0, lanes(dr))
    half = low_ref.shape[0]
    low = dr.astype(BF16)
    low_ref[...] = low[:half]
    high_ref[...] = low[half:]


def attend_back_body(first, per_group, *refs):
    dr1_ref = refs[0]
    pieces = refs[1:9]
    ctx_low_ref, ctx_high_ref, qkv_ref, lse_ref, x_ref, seg_ref, w_ref, wo_ref, vec_ref = refs[9:18]
    refs = refs[18:]
    if first:
        _, dx_ref, gqkv_ref, gout_ref, acc_ref = refs
    else:
        r2_ref, mi2_ref, prev_ref, dx_ref, gqkv_ref, gout_ref, acc_ref, st_ref = refs
    groups = wo_ref.shape[0]
    width = dr1_ref.shape[0]
    size = width // per_group
    scale = size ** (-0.5)
    ctx = jnp.concatenate([ctx_low_ref[...], ctx_high_ref[...]], axis=0)
    dctx = None
    for g in range(groups):
        dal = jnp.concatenate([pieces[2 * g][...], pieces[2 * g + 1][...]], axis=0)
        accumulate(gout_ref, g, nt(ctx, dal))
        term = nn(wo_ref[g], dal)
        dctx = term if dctx is None else dctx + term
    dctx = dctx.astype(BF16)
    x = x_ref[...].astype(BF16)
    query_rows, key_rows = segment_rows(seg_ref[0])
    zero_rows = jnp.zeros_like(query_rows)
    q = qkv_ref[0:width]
    k = qkv_ref[width : 2 * width]
    v = qkv_ref[2 * width : 3 * width]
    dq, dk, dv = [], [], []
    for h in range(per_group):
        part = slice(h * size, (h + 1) * size)
        qh, kh, vh, dch = q[part], k[part], v[part], dctx[part]
        qs = qh * jnp.asarray(scale, BF16)
        delta = jnp.sum(dch.astype(F32) * ctx[part].astype(F32), axis=0, keepdims=True)
        qa = jnp.concatenate([qs, with_rows(query_rows, lse_ref[h : h + 1])], axis=0)
        ka = jnp.concatenate([kh, key_rows], axis=0)
        da = jnp.concatenate([dch, with_rows(zero_rows, delta)], axis=0)
        va = jnp.concatenate([vh, key_rows], axis=0)
        p = jnp.exp(tn(ka, qa))
        ds = (p * tn(va, da)).astype(BF16)
        dv.append(nt(dch, p.astype(BF16)))
        dq.append(nn(kh, ds) * scale)
        dk.append(nt(qs, ds))
    dq = jnp.concatenate(dq, axis=0)
    dk = jnp.concatenate(dk, axis=0)
    dv = jnp.concatenate(dv, axis=0)
    accumulate(acc_ref, 0, lanes(dq))
    accumulate(acc_ref, 1, lanes(dv))
    dx = dr1_ref[...]
    for at, grad in enumerate((dq, dk, dv)):
        low = grad.astype(BF16)
        accumulate(gqkv_ref, at, nt(x, low))
        dx = dx + nn(w_ref[at], low)
    dx_ref[...] = dx
    if not first:
        prev = prev_ref[...]
        nup = prev.shape[1] - 8
        mi2 = mi2_ref[...]
        n2 = (r2_ref[...] - mi2[0:1]) * mi2[1:2]
        e = dx * prev[:, 6 + nup : 7 + nup]
        st_ref[...] = col_sums(e, e * n2)
        accumulate(acc_ref, 2, lanes(dx * n2))
        accumulate(acc_ref, 3, lanes(dx))


class Spec:
    def __init__(self, length, count, offset):
        self.length, self.count, self.offset = length, count, offset

    def tok(self, rows):
        return pl.BlockSpec((rows, self.length), lambda i: (0, i))

    def far(self, rows):
        offset = self.offset
        return pl.BlockSpec((rows, self.length), lambda i: (0, i + offset))

    def seg(self):
        offset = self.offset
        return pl.BlockSpec((1, 1, self.length), lambda i: (i + offset, 0, 0))

    def whole(self, shape):
        return pl.BlockSpec(shape, lambda i: (0,) * len(shape))

    def shape(self, rows, dtype=F32):
        return jax.ShapeDtypeStruct((rows, self.length * self.count), dtype)

    def call(self, body, name, operands, specs, outs, out_specs, flops, aliases=None):
        tokens = self.length * self.count
        moved = sum(math.prod(s.block_shape) * 4 * self.count for s in specs + out_specs if s.block_shape)
        return pl.pallas_call(
            body,
            grid=(self.count,),
            in_specs=specs,
            out_specs=out_specs,
            out_shape=outs,
            name=name,
            input_output_aliases=aliases or {},
            compiler_params=pltpu.CompilerParams(vmem_limit_bytes=VMEM_LIMIT),
            cost_estimate=pl.CostEstimate(
                flops=int(flops * tokens), bytes_accessed=moved, transcendentals=0
            ),
        )(*operands)


def peer(value, step, groups):
    return lax.ppermute(value, "grp", [(i, i ^ step) for i in range(groups)])


def exchange(stats, groups):
    return [stats] + [peer(stats, step, groups) for step in range(1, groups)]


def spread(low, high, groups):
    low_1 = peer(low, 1, groups)
    high_2 = peer(high, 2, groups)
    low_2 = peer(low, 2, groups)
    low_3 = peer(low_1, 2, groups)
    high_1 = peer(high, 1, groups)
    high_3 = peer(high_2, 1, groups)
    return [low, high, low_1, high_1, low_2, high_2, low_3, high_3]


def adam_step(param, grad, first, second, decay, rate):
    first_new = BETA_ONE * first + (1.0 - BETA_ONE) * grad
    second_new = BETA_TWO * second + (1.0 - BETA_TWO) * grad * grad
    first_hat = first_new / (1.0 - BETA_ONE**STEP)
    second_hat = second_new / (1.0 - BETA_TWO**STEP)
    updated = param - rate * (first_hat / (jnp.sqrt(second_hat) + ADAM_EPSILON) + decay * param)
    return (updated, first_new, second_new)


def shards(
    tokens,
    segments,
    owners,
    masters,
    first_moment,
    second_moment,
    vectors,
    vector_first,
    vector_second,
    cotangent,
):
    groups = lax.axis_size("grp")
    me = lax.axis_index("grp")
    capacity = masters.shape[1]
    width, tokens_here = tokens.shape
    full = float(width * groups)
    sequences, length = segments.shape
    per_group = HEADS // groups
    half = width // 2
    nv = vectors.shape[1]
    nup = nv - 8
    per_layer = 3 + 3 * groups
    segs = segments.reshape(sequences, 1, length)

    block_index = slot_index(owners, groups, LAYERS, capacity)
    local_blocks = masters[0].reshape(capacity, width, width).astype(BF16)
    everyone = lax.all_gather(local_blocks, "row", axis=0, tiled=True)
    blocks = jnp.take(everyone, block_index, axis=0).reshape(LAYERS, per_layer, width, width)
    order = jnp.array([0, 1, 2, 3], jnp.int32) ^ me
    w_qkv = [blocks[l, :3] for l in range(LAYERS)]
    w_row = [jnp.take(blocks[l, 3 : 3 + groups], order, axis=0) for l in range(LAYERS)]
    w_up = [blocks[l, 3 + groups : 3 + 2 * groups] for l in range(LAYERS)]
    w_down = [blocks[l, 3 + 2 * groups :] for l in range(LAYERS)]
    w_col = []
    for l in range(LAYERS):
        parts = [w_row[l][0]] + [peer(w_row[l][step], step, groups) for step in range(1, groups)]
        w_col.append(jnp.stack(parts))
    vecs = [vectors[l].T for l in range(LAYERS)]

    cut = (sequences + 1) // 2
    chunks = [Spec(length, cut, 0), Spec(length, sequences - cut, cut)]
    n_chunks = len(chunks)

    keep = [dict() for _ in range(n_chunks)]
    r2 = [None] * n_chunks
    st2 = [None] * n_chunks
    for l in range(LAYERS):
        for c, sp in enumerate(chunks):
            kp = keep[c]
            wspec = sp.whole((3, width, width))
            vspec = sp.whole((width, nv))
            outs = [sp.shape(3 * width, BF16), sp.shape(half, BF16), sp.shape(half, BF16), sp.shape(per_group)]
            out_specs = [sp.tok(3 * width), sp.tok(half), sp.tok(half), sp.tok(per_group)]
            flops = 6 * width * width + 4 * width * length
            body = functools.partial(attend_body, l == 0, per_group, full)
            if l == 0:
                res = sp.call(
                    body, "attend_first", (tokens, segs, w_qkv[l], vecs[l]),
                    [sp.far(width), sp.seg(), wspec, vspec], outs, out_specs, flops,
                )
            else:
                res = sp.call(
                    body, "attend_next", (r2[c], *st2[c], vecs[l - 1], segs, w_qkv[l], vecs[l]),
                    [sp.tok(width)] + [sp.tok(2)] * 4 + [vspec, sp.seg(), wspec, vspec],
                    [sp.shape(width), sp.shape(2)] + outs, [sp.tok(width), sp.tok(2)] + out_specs, flops,
                )
                kp["x", l], kp["mi2", l - 1] = res[:2]
                res = res[2:]
            kp["qkv", l], kp["low", l], kp["high", l], kp["lse", l] = res
            kp["ctx", l] = spread(kp["low", l], kp["high", l], groups)
        for c, sp in enumerate(chunks):
            kp = keep[c]
            x_spec = sp.far(width) if l == 0 else sp.tok(width)
            x = tokens if l == 0 else kp["x", l]
            r1, st1 = sp.call(
                out_body, "out_conv", (x, *kp["ctx", l], w_col[l], vecs[l]),
                [x_spec] + [sp.tok(half)] * 8 + [sp.whole((groups, width, width)), sp.whole((width, nv))],
                [sp.shape(width), sp.shape(2)], [sp.tok(width), sp.tok(2)], 2 * width * width * groups,
            )
            kp["r1", l] = r1
            kp["st1", l] = exchange(st1, groups)
        for c, sp in enumerate(chunks):
            kp = keep[c]
            gw = sp.whole((groups, width, width))
            fg = groups * width
            r2[c], kp["mi1", l], kp["hid", l], kp["gp", l], st = sp.call(
                functools.partial(mlp_body, full), "mlp",
                (kp["r1", l], *kp["st1", l], w_up[l], w_down[l], vecs[l]),
                [sp.tok(width)] + [sp.tok(2)] * 4 + [gw, gw, sp.whole((width, nv))],
                [sp.shape(width), sp.shape(2), sp.shape(fg, BF16), sp.shape(fg, BF16), sp.shape(2)],
                [sp.tok(width), sp.tok(2), sp.tok(fg), sp.tok(fg), sp.tok(2)], 4 * width * width * groups,
            )
            kp["r2", l] = r2[c]
            st2[c] = exchange(st, groups)

    layer_output = jnp.zeros((width, tokens_here), F32)
    input_grad = jnp.zeros((width, tokens_here), F32)
    top = LAYERS - 1
    back = [None] * n_chunks
    flowing = [None] * n_chunks
    norm_acc = [[None] * n_chunks for _ in range(LAYERS)]
    for c, sp in enumerate(chunks):
        kp = keep[c]
        layer_output, kp["mi2", top], st, norm_acc[top][c] = sp.call(
            functools.partial(last_body, full), "last_norm",
            (r2[c], *st2[c], cotangent, vecs[top], layer_output),
            [sp.tok(width)] + [sp.tok(2)] * 4
            + [sp.far(width), sp.whole((width, nv)), pl.BlockSpec(memory_space=pl.ANY)],
            [jax.ShapeDtypeStruct((width, tokens_here), F32), sp.shape(2), sp.shape(2),
             jax.ShapeDtypeStruct((2, width, LANES), F32)],
            [sp.far(width), sp.tok(2), sp.tok(2), sp.whole((2, width, LANES))], 10 * width,
            aliases={7: 0},
        )
        back[c] = exchange(st, groups)
        flowing[c] = cotangent

    block_grads = [None] * LAYERS
    vector_grads = [None] * LAYERS
    acc_mlp = [[None] * n_chunks for _ in range(LAYERS)]
    acc_bo = [[None] * n_chunks for _ in range(LAYERS)]
    acc_att = [[None] * n_chunks for _ in range(LAYERS)]
    summed = [None] * LAYERS
    for l in reversed(range(LAYERS)):
        g_up, g_down, g_qkv, g_out = ([None] * n_chunks for _ in range(4))
        for c, sp in enumerate(chunks):
            kp = keep[c]
            gw = sp.whole((groups, width, width))
            vspec = sp.whole((width, nv))
            fg = groups * width
            kp["dy1", l], st, g_up[c], g_down[c], acc_mlp[l][c] = sp.call(
                functools.partial(mlp_back_body, full), "mlp_back",
                (flowing[c], kp["r2", l], kp["mi2", l], *back[c], kp["r1", l], kp["mi1", l],
                 kp["hid", l], kp["gp", l], w_up[l], w_down[l], vecs[l]),
                [sp.far(width) if l == top else sp.tok(width), sp.tok(width), sp.tok(2)] + [sp.tok(2)] * 4
                + [sp.tok(width), sp.tok(2), sp.tok(fg), sp.tok(fg), gw, gw, vspec],
                [sp.shape(width), sp.shape(2), jax.ShapeDtypeStruct((groups, width, width), F32),
                 jax.ShapeDtypeStruct((groups, width, width), F32),
                 jax.ShapeDtypeStruct((groups + 3, width, LANES), F32)],
                [sp.tok(width), sp.tok(2), gw, gw, sp.whole((groups + 3, width, LANES))],
                8 * width * width * groups,
            )
            back[c] = exchange(st, groups)
        for c, sp in enumerate(chunks):
            kp = keep[c]
            kp["dr1", l], low, high, acc_bo[l][c] = sp.call(
                functools.partial(norm_back_body, full), "norm_back",
                (kp["dy1", l], kp["r1", l], kp["mi1", l], *back[c], vecs[l]),
                [sp.tok(width), sp.tok(width), sp.tok(2)] + [sp.tok(2)] * 4 + [sp.whole((width, nv))],
                [sp.shape(width), sp.shape(half, BF16), sp.shape(half, BF16),
                 jax.ShapeDtypeStruct((1, width, LANES), F32)],
                [sp.tok(width), sp.tok(half), sp.tok(half), sp.whole((1, width, LANES))], 10 * width,
            )
            kp["dal", l] = spread(low, high, groups)
        for c, sp in enumerate(chunks):
            kp = keep[c]
            gw = sp.whole((groups, width, width))
            w3 = sp.whole((3, width, width))
            vspec = sp.whole((width, nv))
            rows = 2 if l == 0 else 4
            operands = [kp["dr1", l], *kp["dal", l], kp["low", l], kp["high", l], kp["qkv", l], kp["lse", l],
                        tokens if l == 0 else kp["x", l], segs, w_qkv[l], w_row[l], vecs[l]]
            specs = [sp.tok(width)] + [sp.tok(half)] * 10 + [
                sp.tok(3 * width), sp.tok(per_group), sp.far(width) if l == 0 else sp.tok(width),
                sp.seg(), w3, gw, vspec]
            outs = [sp.shape(width), jax.ShapeDtypeStruct((3, width, width), F32),
                    jax.ShapeDtypeStruct((groups, width, width), F32),
                    jax.ShapeDtypeStruct((rows, width, LANES), F32)]
            out_specs = [sp.tok(width), w3, gw, sp.whole((rows, width, LANES))]
            aliases = None
            if l == 0:
                operands.append(input_grad)
                specs.append(pl.BlockSpec(memory_space=pl.ANY))
                outs[0] = jax.ShapeDtypeStruct((width, tokens_here), F32)
                out_specs[0] = sp.far(width)
                aliases = {len(operands) - 1: 0}
            else:
                operands += [kp["r2", l - 1], kp["mi2", l - 1], vecs[l - 1]]
                specs += [sp.tok(width), sp.tok(2), vspec]
                outs.append(sp.shape(2))
                out_specs.append(sp.tok(2))
            res = sp.call(
                functools.partial(attend_back_body, l == 0, per_group),
                "attend_back_first" if l == 0 else "attend_back_next", tuple(operands), specs, outs, out_specs,
                4 * width * width * groups + 12 * width * width + 10 * width * length, aliases,
            )
            if l == 0:
                input_grad, g_qkv[c], g_out[c], acc_att[l][c] = res
            else:
                flowing[c], g_qkv[c], g_out[c], acc_att[l][c], st = res
                norm_acc[l - 1][c] = acc_att[l][c][2:4]
                back[c] = exchange(st, groups)
        own_out = sum(g_out)
        inverse_order = order
        own_out = jnp.take(own_out, inverse_order, axis=0)
        grads = jnp.concatenate([sum(g_qkv), own_out, sum(g_up), sum(g_down)], axis=0)
        block_grads[l] = grads

    for l in range(LAYERS):
        def over(parts):
            return jnp.sum(sum(parts), axis=-1)

        att, bo, mlp, norm2 = over(acc_att[l]), over(acc_bo[l]), over(acc_mlp[l]), over(norm_acc[l])
        vector_grads[l] = jnp.concatenate(
            [att[0:2], bo, mlp[0:groups], mlp[groups:], norm2], axis=0
        )
        table = jnp.zeros((1, width, width), F32).at[0, :nv].set(vector_grads[l])
        summed[l] = lax.psum(jnp.concatenate([block_grads[l], table], axis=0).astype(BF16), "row")

    summed_blocks = jnp.concatenate([s[:per_layer] for s in summed], axis=0)
    summed_vectors = jnp.stack([s[per_layer, :nv] for s in summed], axis=0).astype(F32)
    flat = summed_blocks.reshape(LAYERS * per_layer, width * width)
    own_row = lax.axis_index("row")
    targets = own_row * capacity + jnp.arange(capacity, dtype=jnp.int32)
    selector = (block_index[None, :] == targets[:, None]).astype(BF16)
    own_grads = jnp.dot(selector, flat, preferred_element_type=F32)[None]
    new_masters, new_first, new_second = adam_step(
        masters, own_grads, first_moment, second_moment, WEIGHT_DECAY, LEARN_RATE
    )
    new_vectors, new_vector_first, new_vector_second = adam_step(
        vectors, summed_vectors, vector_first, vector_second, 0.0, VECTOR_RATE
    )
    return (
        layer_output,
        input_grad,
        new_masters,
        new_first,
        new_second,
        new_vectors,
        new_vector_first,
        new_vector_second,
    )


def solution(mesh):
    in_specs = (
        P("grp", "row"),
        P("row", None),
        P(),
        P("grp", "row", None),
        P("grp", "row", None),
        P("grp", "row", None),
        P(None, None, "grp"),
        P(None, None, "grp"),
        P(None, None, "grp"),
        P("grp", "row"),
    )
    out_specs = (
        P("grp", "row"),
        P("grp", "row"),
        P("grp", "row", None),
        P("grp", "row", None),
        P("grp", "row", None),
        P(None, None, "grp"),
        P(None, None, "grp"),
        P(None, None, "grp"),
    )
    return jax.shard_map(shards, mesh=mesh, in_specs=in_specs, out_specs=out_specs, check_vma=False)
```

time: 1060 us -> 606 us (0.57)
  matrix products: 285 us -> 5.67 us
  Pallas kernels: 0 us -> 174 us
  blocking collectives: 155 us -> 0 us
  waiting for transfers between devices: 341 us -> 209 us
  local copies, waits for them, and re-layouts: 182 us -> 62.8 us
  starting transfers between devices: 0.46 us -> 113 us
  other arithmetic: 62.1 us -> 16.1 us
    dot_general x107 -> x1, matrix products: 285 us -> 5.67 us  [shards(): own_grads = jnp.dot(selector, flat, preferred_element_type=F32)[None]]
    pallas_call x0 -> x26, Pallas kernels: none -> 174 us  [call(): pl.pallas_call(body, grid=(self.count,), in_specs=specs, out_specs=out_sp...]
    reduce_scatter x2 -> x0, waiting for transfers between devices: 157 us -> none  [layer_forward(): mixed = lax.psum_scatter(out_terms, 'grp', scatter_dimension=1, tiled=True)]
    psum x9 -> x0, blocking collectives: 155 us -> none  [the longest x4 64.4 us: normalize(): lax.psum((jnp.sum(resid, axis=1), jnp.sum(resid * resid, axis=1)), 'grp')]
    ppermute x0 -> x102, starting transfers between devices: none -> 113 us  [peer(): return lax.ppermute(value, 'grp', [(i, i ^ step) for i in range(groups)])]
    ppermute x0 -> x102, waiting for transfers between devices: none -> 67.2 us  [peer(): return lax.ppermute(value, 'grp', [(i, i ^ step) for i in range(groups)])]
    concatenate x15 -> x2, local copies, waits for them, and re-layouts: 57.8 us -> 0.65 us  [shards(): jnp.concatenate([block_grads[l], table], axis=0).astype(BF16)]
    all_gather x3 -> x1, waiting for transfers between devices: 115 us -> 66.9 us  [shards(): everyone = lax.all_gather(local_blocks, 'row', axis=0, tiled=True)]
  transfers between devices with their start and end apart: 6 -> 104, of which waited for: 5 -> 24; matrix products, arithmetic and copies ran while one was open for 7% -> 2% of each run, Pallas kernels for 0% -> 24%
where the time goes in v1:
time: 606 us; the launch traced here: 597 us
  waiting for transfers between devices  209 us (34%)
  Pallas kernels  174 us (29%)
  starting transfers between devices  113 us (19%)
  local copies, waits for them, and re-layouts  62.8 us (10%)
  other arithmetic  16.1 us (3%)
  between operations  15.7 us (3%)
    pallas_call x26, Pallas kernels, call(): pl.pallas_call(body, grid=(self.count,), in_specs=specs, out_specs=out_sp...  174 us
    ppermute x102, starting transfers between devices, peer(): return lax.ppermute(value, 'grp', [(i, i ^ step) for i in range(groups)])  113 us
    psum x1, waiting for transfers between devices, shards(): lax.psum(jnp.concatenate([block_grads[l], table], axis=0).astype(BF16), '...  75.1 us
    ppermute x102, waiting for transfers between devices, peer(): return lax.ppermute(value, 'grp', [(i, i ^ step) for i in range(groups)])  67.2 us
    all_gather x1, waiting for transfers between devices, shards(): everyone = lax.all_gather(local_blocks, 'row', axis=0, tiled=True)  66.9 us
    unnamed x237, local copies, waits for them, and re-layouts  34.6 us
  transfers between devices with their start and end apart: 104, of which 24 were waited for; matrix products, arithmetic and copies ran while one was open for 2% of the time, Pallas kernels for 24%

profile of v1, /device:TPU:0, one launch (start us, length us, event | category | flops | bytes accessed | tf_op | source)
XLA Modules:
  0.0 596.5 jit_solution(8958896443604122526)
XLA Ops:
  11.1 66.9 %all-gather.2.cloned.1.call-done = bf16[64,192,192]{2,1,0:T(8,128)(2,1)} async-done(((bf16[8,192,192]{2,1,0:T(8,128)(2,1)}), bf16[64,192,192]{2,1,0:T(8,128)(2,1)}) %all-gather.2.cloned.1.call-update) | async-done | bytes 4718608 | tf_op jit(solution)/shard_map/all_gather | solution.py:469
  78.0 5.1 gather_fusion
  90.8 8.8 %attend_first.3 = (bf16[576,1536]{1,0:T(8,128)(2,1)S(1)}, bf16[96,1536]{1,0:T(8,128)(2,1)S(1)}, bf16[96,1536]{1,0:T(8,128)(2,1)S(1)}, f32[3,1536]{1,0:T(4,128)S(1)}) custom-call(bf16[192,2560]{1,0:T(8,128)(2,1)S(1)} %copy-done.1, s32[5,1,512]{2,1,0:T(1,128)S(1)} %reshape.132.refs_1_.refs_6_.refs_14_, ...), custom_call_target="tpu_custom_call" | custom-call | flops 943718400 | bytes 7277568 | tf_op jit(solution)/shard_map/attend_first/pallas_call | solution.py:400
  105.1 6.5 %attend_first.2 = (bf16[576,1024]{1,0:T(8,128)(2,1)S(1)}, bf16[96,1024]{1,0:T(8,128)(2,1)}, bf16[96,1024]{1,0:T(8,128)(2,1)}, f32[3,1024]{1,0:T(4,128)S(1)}) custom-call(bf16[192,2560]{1,0:T(8,128)(2,1)S(1)} %copy-done.1, s32[5,1,512]{2,1,0:T(1,128)S(1)} %reshape.132.refs_1_.refs_6_.refs_14_, bf16[3,192,192]{2,1,0:T(8,128)(2,1)S(1)} %copy-done.17, ...), custom_call_target="tpu_custom_call" | custom-call | flops 629145600 | bytes 4851712 | tf_op jit(solution)/shard_map/attend_first/pallas_call | solution.py:400
  116.8 5.0 collective-permute-done.6
  128.1 13.1 %collective-permute-done.3.refs_5_ = bf16[96,1024]{1,0:T(8,128)(2,1)} collective-permute-done((bf16[96,1024]{1,0:T(8,128)(2,1)}, bf16[96,1024]{1,0:T(8,128)(2,1)}, u32[]{:S(2)}, u32[]{:S(2)}) %collective-permute-start.3) | collective-permute-done | bytes 196640 | tf_op jit(solution)/shard_map/ppermute | solution.py:416
  154.4 2.9 out_conv.6
  166.7 9.0 %mlp.6 = (f32[192,1536]{1,0:T(8,128)S(1)}, f32[2,1536]{1,0:T(2,128)S(1)}, bf16[768,1536]{1,0:T(8,128)(2,1)S(1)}, bf16[768,1536]{1,0:T(8,128)(2,1)}, f32[2,1536]{1,0:T(2,128)S(1)}) custom-call(f32[192,1536]{1,0:T(8,128)S(1)} %get-tuple-element.159.r1_ref, f32[2,1536]{1,0:T(2,128)S(1)} %get-tuple-element.160.s0, f32[2,1536]{1,0:T(2,128)S(1)} %collective-permute-done.36.s1, ...), custom_call_target="tpu_custom_call" | custom-call | flops 905969664 | bytes 15436800 | tf_op jit(solution)/shard_map/mlp/pallas_call | solution.py:400
  180.6 5.8 mlp.4
  192.2 9.3 %attend_next.3 = (f32[192,1536]{1,0:T(8,128)S(1)}, f32[2,1536]{1,0:T(2,128)S(1)}, bf16[576,1536]{1,0:T(8,128)(2,1)S(1)}, bf16[96,1536]{1,0:T(8,128)(2,1)S(1)}, b...) custom-call(f32[192,1536]{1,0:T(8,128)S(1)} %get-tuple-element.161.refs_0_.refs_18_.r2_ref, ...), custom_call_target="tpu_custom_call" | custom-call | flops 943718400 | bytes 8546304 | tf_op jit(solution)/shard_map/attend_next/pallas_call | solution.py:400
  207.5 6.2 %attend_next.2 = (f32[192,1024]{1,0:T(8,128)S(1)}, f32[2,1024]{1,0:T(2,128)S(1)}, bf16[576,1024]{1,0:T(8,128)(2,1)S(1)}, bf16[96,1024]{1,0:T(8,128)(2,1)S(1)}, b...) custom-call(f32[192,1024]{1,0:T(8,128)S(1)} %get-tuple-element.148.refs_0_.refs_18_.r2_ref, ...), custom_call_target="tpu_custom_call" | custom-call | flops 629145600 | bytes 5697536 | tf_op jit(solution)/shard_map/attend_next/pallas_call | solution.py:400
  218.9 3.3 collective-permute-done.22
  228.7 12.9 %collective-permute-done.18.refs_5_ = bf16[96,1024]{1,0:T(8,128)(2,1)S(1)} collective-permute-done((bf16[96,1024]{1,0:T(8,128)(2,1)S(1)}, bf16[96,1024]{1,0:T(8,128)(2,1)S(1)}, u32[]{:S(2)}, u32[]{:S(2)}) %collective-permute-start.18) | collective-permute-done | bytes 196640 | tf_op jit(solution)/shard_map/ppermute | solution.py:416
  248.6 2.5 collective-permute-start.50
  255.8 9.4 %mlp.7 = (f32[192,1536]{1,0:T(8,128)S(1)}, f32[2,1536]{1,0:T(2,128)S(1)}, bf16[768,1536]{1,0:T(8,128)(2,1)S(1)}, bf16[768,1536]{1,0:T(8,128)(2,1)}, f32[2,1536]{1,0:T(2,128)S(1)}) custom-call(f32[192,1536]{1,0:T(8,128)S(1)} %get-tuple-element.166.r1_ref, f32[2,1536]{1,0:T(2,128)S(1)} %get-tuple-element.167.s0, f32[2,1536]{1,0:T(2,128)S(1)} %collective-permute-done.48.s1, ...), custom_call_target="tpu_custom_call" | custom-call | flops 905969664 | bytes 15436800 | tf_op jit(solution)/shard_map/mlp/pallas_call | solution.py:400
  270.1 5.5 mlp.5
  292.4 8.9 %mlp_back.4 = (f32[192,1024]{1,0:T(8,128)S(1)}, f32[2,1024]{1,0:T(2,128)S(1)}, f32[4,192,192]{2,1,0:T(8,128)S(1)}, f32[4,192,192]{2,1,0:T(8,128)S(1)}, f32[7,192,128]{2,1,0:T(8,128)S(1)}) custom-call(f32[192,2560]{1,0:T(8,128)} %dy_ref.3, f32[192,1024]{1,0:T(8,128)S(1)} %get-tuple-element.155.r2_ref, f32[2,1024]{1,0:T(2,128)S(1)} %get-tuple-element.172.mi2_ref, ...), custom_call_target="tpu_custom_call" | custom-call | flops 1207959552 | bytes 15607808 | tf_op jit(solution)/shard_map/mlp_back/pallas_call | solution.py:400
  319.9 13.1 %mlp_back.6 = (f32[192,1536]{1,0:T(8,128)S(1)}, f32[2,1536]{1,0:T(2,128)S(1)}, f32[4,192,192]{2,1,0:T(8,128)S(1)}, f32[4,192,192]{2,1,0:T(8,128)S(1)}, f32[7,192,128]{2,1,0:T(8,128)S(1)}) custom-call(f32[192,2560]{1,0:T(8,128)} %dy_ref.3, f32[192,1536]{1,0:T(8,128)S(1)} %get-tuple-element.168.r2_ref, f32[2,1536]{1,0:T(2,128)S(1)} %get-tuple-element.197.mi2_ref, ...), custom_call_target="tpu_custom_call" | custom-call | flops 1811939328 | bytes 23411712 | tf_op jit(solution)/shard_map/mlp_back/pallas_call | solution.py:400
  335.3 3.2 collective-permute-done.81.s1
  339.1 3.1 collective-permute-done.82.s2
  343.6 3.4 collective-permute-done.83.s3
  349.9 10.7 %attend_back_next.2 = (f32[192,1024]{1,0:T(8,128)S(1)}, f32[3,192,192]{2,1,0:T(8,128)S(1)}, f32[4,192,192]{2,1,0:T(8,128)S(1)}, f32[4,192,128]{2,1,0:T(8,128)S(1)}, f32[2,1024]{1,0:T(2,128)S(1)}) custom-call(f32[192,1024]{1,0:T(8,128)} %copy-done.84, bf16[96,1024]{1,0:T(8,128)(2,1)S(1)} %get-tuple-element.180.refs_1_, ...), custom_call_target="tpu_custom_call" | custom-call | flops 2063597568 | bytes 14422016 | tf_op jit(solution)/shard_map/attend_back_next/pallas_call | solution.py:400
  367.0 5.9 collective-permute-done.67.s2
  374.7 2.7 collective-permute-done.68.s3
  377.4 9.0 %mlp_back.5 = (f32[192,1024]{1,0:T(8,128)S(1)}, f32[2,1024]{1,0:T(2,128)S(1)}, f32[4,192,192]{2,1,0:T(8,128)S(1)}, f32[4,192,192]{2,1,0:T(8,128)S(1)}, f32[7,192,128]{2,1,0:T(8,128)S(1)}) custom-call(f32[192,1024]{1,0:T(8,128)S(1)} %get-tuple-element.185.dy_ref, f32[192,1024]{1,0:T(8,128)S(1)} %copy-done.23, ...), custom_call_target="tpu_custom_call" | custom-call | flops 1207959552 | bytes 15607808 | tf_op jit(solution)/shard_map/mlp_back/pallas_call | solution.py:400
  392.7 16.2 %attend_back_next.3 = (f32[192,1536]{1,0:T(8,128)}, f32[3,192,192]{2,1,0:T(8,128)S(1)}, f32[4,192,192]{2,1,0:T(8,128)S(1)}, f32[4,192,128]{2,1,0:T(8,128)S(1)}, f32[2,1536]{1,0:T(2,128)S(1)}) custom-call(f32[192,1536]{1,0:T(8,128)} %copy-done.82, bf16[96,1536]{1,0:T(8,128)(2,1)S(1)} %get-tuple-element.205.refs_1_, ...), custom_call_target="tpu_custom_call" | custom-call | flops 3095396352 | bytes 21633024 | tf_op jit(solution)/shard_map/attend_back_next/pallas_call | solution.py:400
  415.9 13.2 %mlp_back.7 = (f32[192,1536]{1,0:T(8,128)S(1)}, f32[2,1536]{1,0:T(2,128)S(1)}, f32[4,192,192]{2,1,0:T(8,128)S(1)}, f32[4,192,192]{2,1,0:T(8,128)S(1)}, f32[7,192,128]{2,1,0:T(8,128)S(1)}) custom-call(f32[192,1536]{1,0:T(8,128)S(1)} %copy-done.21, f32[192,1536]{1,0:T(8,128)} %copy-done.19, f32[2,1536]{1,0:T(2,128)S(1)} %copy-done.81, ...), custom_call_target="tpu_custom_call" | custom-call | flops 1811939328 | bytes 23411712 | tf_op jit(solution)/shard_map/mlp_back/pallas_call | solution.py:400
  462.1 16.1 %attend_back_first.2 = (f32[192,2560]{1,0:T(8,128)}, f32[3,192,192]{2,1,0:T(8,128)S(1)}, f32[4,192,192]{2,1,0:T(8,128)S(1)}, f32[2,192,128]{2,1,0:T(8,128)S(1)}) custom-call(f32[192,1536]{1,0:T(8,128)} %copy-done.83, bf16[96,1536]{1,0:T(8,128)(2,1)} %get-tuple-element.218.refs_1_, ...), custom_call_target="tpu_custom_call", output_to_operand_aliasing={{0}: (18, {})} | custom-call | flops 3095396352 | bytes 19811328 | tf_op jit(solution)/shard_map/attend_back_first/pallas_call | solution.py:400
  478.3 11.3 %attend_back_first.3 = (f32[192,2560]{1,0:T(8,128)}, f32[3,192,192]{2,1,0:T(8,128)S(1)}, f32[4,192,192]{2,1,0:T(8,128)S(1)}, f32[2,192,128]{2,1,0:T(8,128)S(1)}) custom-call(f32[192,1024]{1,0:T(8,128)S(1)} %get-tuple-element.192.refs_0_, bf16[96,1024]{1,0:T(8,128)(2,1)S(1)} %copy-done.67, ...), custom_call_target="tpu_custom_call", output_to_operand_aliasing={{0}: (18, {})} | custom-call | flops 2063597568 | bytes 13207552 | tf_op jit(solution)/shard_map/attend_back_first/pallas_call | solution.py:400
  498.2 75.1 %all-reduce.5.cloned.1.call-done = (bf16[16,192,192]{2,1,0:T(8,128)(2,1)}, bf16[16,192,192]{2,1,0:T(8,128)(2,1)}) async-done(((bf16[16,192,192]{2,1,0:T(8,128)(2,1)}, bf16[16,192,192]{2,1,0:T(8,128)(2,1)}), (bf16[16,192,192]{2,1,0:T(8,128)(2,1)}, bf16[16,192,192]{2,1,0:T(8,128)(2,1)})) %all-reduce.5.cloned.1.call-update) | async-done | bytes 2359312 | tf_op jit(solution)/shard_map/psum | solution.py:649
  578.8 4.8 reshape.135
  583.6 5.7 multiply_subtract_fusion
  (502 shorter events, 206.4 us)
Async XLA Ops:
  7.2 70.8 %all-gather.2.cloned.1.call-start = ((), (), s32[]{:S(2)}) async-start(), calls=%async_computation | async-start | bytes 7077888 | tf_op jit(solution)/shard_map/all_gather | solution.py:469
  10.4 562.8 %all-reduce.5.cloned.1.call-start = ((), (), s32[]{:S(2)}) async-start(), calls=%async_computation.1 | async-start | bytes 6291456 | tf_op jit(solution)/shard_map/psum | solution.py:649
  100.8 24.0 %collective-permute-start.30 = (bf16[96,1536]{1,0:T(8,128)(2,1)S(1)}, bf16[96,1536]{1,0:T(8,128)(2,1)S(1)}, u32[]{:S(2)}, u32[]{:S(2)}) collective-permute-start(bf16[96,1536]{1,0:T(8,128)(2,1)S(1)} %get-tuple-element.157.refs_0_.refs_9_), channel_id=1, source_target_pairs={{0,8},{8,0},{16,24},{24,16},{1,9},{9,1},{17,25},{25,17},{2,10},{10... | collective-permute-start | bytes 884744 | tf_op jit(solution)/shard_map/ppermute | solution.py:416
  104.6 23.0 %collective-permute-start.33 = (bf16[96,1536]{1,0:T(8,128)(2,1)S(1)}, bf16[96,1536]{1,0:T(8,128)(2,1)}, u32[]{:S(2)}, u32[]{:S(2)}) collective-permute-start(bf16[96,1536]{1,0:T(8,128)(2,1)S(1)} %get-tuple-element.158.refs_1_.refs_10_), channel_id=1, source_target_pairs={{0,16},{8,24},{16,0},{24,8},{1,17},{9,25},{17,1},{25,9},{2,18},{10... | collective-permute-start | bytes 884744 | tf_op jit(solution)/shard_map/ppermute | solution.py:416
  121.8 20.0 %collective-permute-start.31 = (bf16[96,1536]{1,0:T(8,128)(2,1)S(1)}, bf16[96,1536]{1,0:T(8,128)(2,1)S(1)}, u32[]{:S(2)}, u32[]{:S(2)}) collective-permute-start(bf16[96,1536]{1,0:T(8,128)(2,1)S(1)} %get-tuple-element.158.refs_1_.refs_10_), channel_id=1, source_target_pairs={{0,8},{8,0},{16,24},{24,16},{1,9},{9,1},{17,25},{25,17},{2,10},{10... | collective-permute-start | bytes 884744 | tf_op jit(solution)/shard_map/ppermute | solution.py:416
  123.3 20.7 %collective-permute-start.32 = (bf16[96,1536]{1,0:T(8,128)(2,1)S(1)}, bf16[96,1536]{1,0:T(8,128)(2,1)S(1)}, u32[]{:S(2)}, u32[]{:S(2)}) collective-permute-start(bf16[96,1536]{1,0:T(8,128)(2,1)S(1)} %get-tuple-element.157.refs_0_.refs_9_), channel_id=1, source_target_pairs={{0,16},{8,24},{16,0},{24,8},{1,17},{9,25},{17,1},{25,9},{2,18},{10... | collective-permute-start | bytes 884744 | tf_op jit(solution)/shard_map/ppermute | solution.py:416
  124.8 20.4 %collective-permute-start.34 = (bf16[96,1536]{1,0:T(8,128)(2,1)S(1)}, bf16[96,1536]{1,0:T(8,128)(2,1)S(1)}, u32[]{:S(2)}, u32[]{:S(2)}) collective-permute-start(bf16[96,1536]{1,0:T(8,128)(2,1)S(1)} %collective-permute-done.30.refs_2_), channel_id=1, source_target_pairs={{0,16},{8,24},{16,0},{24,8},{1,17},{9,25},{17,1},{25,9},{2,18},{10... | collective-permute-start | bytes 884744 | tf_op jit(solution)/shard_map/ppermute | solution.py:416
  127.6 21.1 %collective-permute-start.35 = (bf16[96,1536]{1,0:T(8,128)(2,1)}, bf16[96,1536]{1,0:T(8,128)(2,1)}, u32[]{:S(2)}, u32[]{:S(2)}) collective-permute-start(bf16[96,1536]{1,0:T(8,128)(2,1)} %collective-permute-done.33.refs_5_), channel_id=1, source_target_pairs={{0,8},{8,0},{16,24},{24,16},{1,9},{9,1},{17,25},{25,17},{2,10},{10... | collective-permute-start | bytes 884744 | tf_op jit(solution)/shard_map/ppermute | solution.py:416
  189.3 18.2 %collective-permute-start.13 = (f32[2,1024]{1,0:T(2,128)S(1)}, f32[2,1024]{1,0:T(2,128)S(1)}, u32[]{:S(2)}, u32[]{:S(2)}) collective-permute-start(f32[2,1024]{1,0:T(2,128)S(1)} %get-tuple-element.149.refs_1_), channel_id=1, source_target_pairs={{0,16},{8,24},{16,0},{24,8},{1,17},{9,25},{17,1},{25,9},{2,18},{10... | collective-permute-start | bytes 24584 | tf_op jit(solution)/shard_map/ppermute | solution.py:416
  203.9 21.8 %collective-permute-start.42 = (bf16[96,1536]{1,0:T(8,128)(2,1)S(1)}, bf16[96,1536]{1,0:T(8,128)(2,1)S(1)}, u32[]{:S(2)}, u32[]{:S(2)}) collective-permute-start(bf16[96,1536]{1,0:T(8,128)(2,1)S(1)} %get-tuple-element.164.refs_0_.refs_9_), channel_id=1, source_target_pairs={{0,8},{8,0},{16,24},{24,16},{1,9},{9,1},{17,25},{25,17},{2,10},{10... | collective-permute-start | bytes 884744 | tf_op jit(solution)/shard_map/ppermute | solution.py:416
  206.1 21.7 %collective-permute-start.45 = (bf16[96,1536]{1,0:T(8,128)(2,1)S(1)}, bf16[96,1536]{1,0:T(8,128)(2,1)S(1)}, u32[]{:S(2)}, u32[]{:S(2)}) collective-permute-start(bf16[96,1536]{1,0:T(8,128)(2,1)S(1)} %get-tuple-element.165.refs_1_.refs_10_), channel_id=1, source_target_pairs={{0,16},{8,24},{16,0},{24,8},{1,17},{9,25},{17,1},{25,9},{2,18},{10... | collective-permute-start | bytes 884744 | tf_op jit(solution)/shard_map/ppermute | solution.py:416
  222.1 19.5 %collective-permute-start.43 = (bf16[96,1536]{1,0:T(8,128)(2,1)S(1)}, bf16[96,1536]{1,0:T(8,128)(2,1)S(1)}, u32[]{:S(2)}, u32[]{:S(2)}) collective-permute-start(bf16[96,1536]{1,0:T(8,128)(2,1)S(1)} %get-tuple-element.165.refs_1_.refs_10_), channel_id=1, source_target_pairs={{0,8},{8,0},{16,24},{24,16},{1,9},{9,1},{17,25},{25,17},{2,10},{10... | collective-permute-start | bytes 884744 | tf_op jit(solution)/shard_map/ppermute | solution.py:416
  223.9 18.8 %collective-permute-start.44 = (bf16[96,1536]{1,0:T(8,128)(2,1)S(1)}, bf16[96,1536]{1,0:T(8,128)(2,1)S(1)}, u32[]{:S(2)}, u32[]{:S(2)}) collective-permute-start(bf16[96,1536]{1,0:T(8,128)(2,1)S(1)} %get-tuple-element.164.refs_0_.refs_9_), channel_id=1, source_target_pairs={{0,16},{8,24},{16,0},{24,8},{1,17},{9,25},{17,1},{25,9},{2,18},{10... | collective-permute-start | bytes 884744 | tf_op jit(solution)/shard_map/ppermute | solution.py:416
  225.7 17.9 %collective-permute-start.46 = (bf16[96,1536]{1,0:T(8,128)(2,1)S(1)}, bf16[96,1536]{1,0:T(8,128)(2,1)S(1)}, u32[]{:S(2)}, u32[]{:S(2)}) collective-permute-start(bf16[96,1536]{1,0:T(8,128)(2,1)S(1)} %collective-permute-done.42.refs_2_), channel_id=1, source_target_pairs={{0,16},{8,24},{16,0},{24,8},{1,17},{9,25},{17,1},{25,9},{2,18},{10... | collective-permute-start | bytes 884744 | tf_op jit(solution)/shard_map/ppermute | solution.py:416
  227.8 18.0 %collective-permute-start.47 = (bf16[96,1536]{1,0:T(8,128)(2,1)S(1)}, bf16[96,1536]{1,0:T(8,128)(2,1)S(1)}, u32[]{:S(2)}, u32[]{:S(2)}) collective-permute-start(bf16[96,1536]{1,0:T(8,128)(2,1)S(1)} %collective-permute-done.45.refs_5_), channel_id=1, source_target_pairs={{0,8},{8,0},{16,24},{24,16},{1,9},{9,1},{17,25},{25,17},{2,10},{10... | collective-permute-start | bytes 884744 | tf_op jit(solution)/shard_map/ppermute | solution.py:416
  252.7 17.4 %collective-permute-start.25 = (f32[2,1024]{1,0:T(2,128)S(1)}, f32[2,1024]{1,0:T(2,128)S(1)}, u32[]{:S(2)}, u32[]{:S(2)}) collective-permute-start(f32[2,1024]{1,0:T(2,128)S(1)} %get-tuple-element.154.s0), channel_id=1, source_target_pairs={{0,16},{8,24},{16,0},{24,8},{1,17},{9,25},{17,1},{25,9},{2,18},{10... | collective-permute-start | bytes 24584 | tf_op jit(solution)/shard_map/ppermute | solution.py:416
  315.8 32.6 %collective-permute-start.61 = (bf16[96,1024]{1,0:T(8,128)(2,1)S(1)}, bf16[96,1024]{1,0:T(8,128)(2,1)S(1)}, u32[]{:S(2)}, u32[]{:S(2)}) collective-permute-start(bf16[96,1024]{1,0:T(8,128)(2,1)S(1)} %get-tuple-element.181.refs_2_), channel_id=1, source_target_pairs={{0,8},{8,0},{16,24},{24,16},{1,9},{9,1},{17,25},{25,17},{2,10},{10... | collective-permute-start | bytes 589832 | tf_op jit(solution)/shard_map/ppermute | solution.py:416
  316.3 33.6 %collective-permute-start.62 = (bf16[96,1024]{1,0:T(8,128)(2,1)S(1)}, bf16[96,1024]{1,0:T(8,128)(2,1)S(1)}, u32[]{:S(2)}, u32[]{:S(2)}) collective-permute-start(bf16[96,1024]{1,0:T(8,128)(2,1)S(1)} %get-tuple-element.180.refs_1_), channel_id=1, source_target_pairs={{0,16},{8,24},{16,0},{24,8},{1,17},{9,25},{17,1},{25,9},{2,18},{10... | collective-permute-start | bytes 589832 | tf_op jit(solution)/shard_map/ppermute | solution.py:416
  317.7 32.1 %collective-permute-start.64 = (bf16[96,1024]{1,0:T(8,128)(2,1)S(1)}, bf16[96,1024]{1,0:T(8,128)(2,1)S(1)}, u32[]{:S(2)}, u32[]{:S(2)}) collective-permute-start(bf16[96,1024]{1,0:T(8,128)(2,1)S(1)} %collective-permute-done.60.refs_3_), channel_id=1, source_target_pairs={{0,16},{8,24},{16,0},{24,8},{1,17},{9,25},{17,1},{25,9},{2,18},{10... | collective-permute-start | bytes 589832 | tf_op jit(solution)/shard_map/ppermute | solution.py:416
  318.3 31.5 %collective-permute-start.65 = (bf16[96,1024]{1,0:T(8,128)(2,1)S(1)}, bf16[96,1024]{1,0:T(8,128)(2,1)S(1)}, u32[]{:S(2)}, u32[]{:S(2)}) collective-permute-start(bf16[96,1024]{1,0:T(8,128)(2,1)S(1)} %collective-permute-done.63.refs_6_), channel_id=1, source_target_pairs={{0,8},{8,0},{16,24},{24,16},{1,9},{9,1},{17,25},{25,17},{2,10},{10... | collective-permute-start | bytes 589832 | tf_op jit(solution)/shard_map/ppermute | solution.py:416
  361.4 28.5 %collective-permute-start.85 = (bf16[96,1536]{1,0:T(8,128)(2,1)S(1)}, bf16[96,1536]{1,0:T(8,128)(2,1)S(1)}, u32[]{:S(2)}, u32[]{:S(2)}) collective-permute-start(bf16[96,1536]{1,0:T(8,128)(2,1)S(1)} %get-tuple-element.206.refs_2_), channel_id=1, source_target_pairs={{0,8},{8,0},{16,24},{24,16},{1,9},{9,1},{17,25},{25,17},{2,10},{10... | collective-permute-start | bytes 884744 | tf_op jit(solution)/shard_map/ppermute | solution.py:416
  362.7 28.6 %collective-permute-start.86 = (bf16[96,1536]{1,0:T(8,128)(2,1)S(1)}, bf16[96,1536]{1,0:T(8,128)(2,1)S(1)}, u32[]{:S(2)}, u32[]{:S(2)}) collective-permute-start(bf16[96,1536]{1,0:T(8,128)(2,1)S(1)} %get-tuple-element.205.refs_1_), channel_id=1, source_target_pairs={{0,16},{8,24},{16,0},{24,8},{1,17},{9,25},{17,1},{25,9},{2,18},{10... | collective-permute-start | bytes 884744 | tf_op jit(solution)/shard_map/ppermute | solution.py:416
  363.3 29.4 %collective-permute-start.88 = (bf16[96,1536]{1,0:T(8,128)(2,1)S(1)}, bf16[96,1536]{1,0:T(8,128)(2,1)S(1)}, u32[]{:S(2)}, u32[]{:S(2)}) collective-permute-start(bf16[96,1536]{1,0:T(8,128)(2,1)S(1)} %collective-permute-done.84.refs_3_), channel_id=1, source_target_pairs={{0,16},{8,24},{16,0},{24,8},{1,17},{9,25},{17,1},{25,9},{2,18},{10... | collective-permute-start | bytes 884744 | tf_op jit(solution)/shard_map/ppermute | solution.py:416
  364.8 27.9 %collective-permute-start.89 = (bf16[96,1536]{1,0:T(8,128)(2,1)S(1)}, bf16[96,1536]{1,0:T(8,128)(2,1)S(1)}, u32[]{:S(2)}, u32[]{:S(2)}) collective-permute-start(bf16[96,1536]{1,0:T(8,128)(2,1)S(1)} %collective-permute-done.87.refs_6_), channel_id=1, source_target_pairs={{0,8},{8,0},{16,24},{24,16},{1,9},{9,1},{17,25},{25,17},{2,10},{10... | collective-permute-start | bytes 884744 | tf_op jit(solution)/shard_map/ppermute | solution.py:416
  389.2 21.9 %collective-permute-start.69 = (f32[2,1024]{1,0:T(2,128)S(1)}, f32[2,1024]{1,0:T(2,128)S(1)}, u32[]{:S(2)}, u32[]{:S(2)}) collective-permute-start(f32[2,1024]{1,0:T(2,128)S(1)} %get-tuple-element.191.s0), channel_id=1, source_target_pairs={{0,8},{8,0},{16,24},{24,16},{1,9},{9,1},{17,25},{25,17},{2,10},{10... | collective-permute-start | bytes 24584 | tf_op jit(solution)/shard_map/ppermute | solution.py:416
  389.8 22.7 %collective-permute-start.70 = (f32[2,1024]{1,0:T(2,128)S(1)}, f32[2,1024]{1,0:T(2,128)S(1)}, u32[]{:S(2)}, u32[]{:S(2)}) collective-permute-start(f32[2,1024]{1,0:T(2,128)S(1)} %get-tuple-element.191.s0), channel_id=1, source_target_pairs={{0,16},{8,24},{16,0},{24,8},{1,17},{9,25},{17,1},{25,9},{2,18},{10... | collective-permute-start | bytes 24584 | tf_op jit(solution)/shard_map/ppermute | solution.py:416
  391.3 21.3 %collective-permute-start.71 = (f32[2,1024]{1,0:T(2,128)S(1)}, f32[2,1024]{1,0:T(2,128)S(1)}, u32[]{:S(2)}, u32[]{:S(2)}) collective-permute-start(f32[2,1024]{1,0:T(2,128)S(1)} %get-tuple-element.191.s0), channel_id=1, source_target_pairs={{0,24},{8,16},{16,8},{24,0},{1,25},{9,17},{17,9},{25,1},{2,26},{10... | collective-permute-start | bytes 24584 | tf_op jit(solution)/shard_map/ppermute | solution.py:416
  413.8 37.0 %collective-permute-start.72 = (bf16[96,1024]{1,0:T(8,128)(2,1)S(1)}, bf16[96,1024]{1,0:T(8,128)(2,1)S(1)}, u32[]{:S(2)}, u32[]{:S(2)}) collective-permute-start(bf16[96,1024]{1,0:T(8,128)(2,1)S(1)} %get-tuple-element.193.refs_1_), channel_id=1, source_target_pairs={{0,8},{8,0},{16,24},{24,16},{1,9},{9,1},{17,25},{25,17},{2,10},{10... | collective-permute-start | bytes 589832 | tf_op jit(solution)/shard_map/ppermute | solution.py:416
  456.5 21.7 %collective-permute-start.73 = (bf16[96,1024]{1,0:T(8,128)(2,1)S(1)}, bf16[96,1024]{1,0:T(8,128)(2,1)S(1)}, u32[]{:S(2)}, u32[]{:S(2)}) collective-permute-start(bf16[96,1024]{1,0:T(8,128)(2,1)S(1)} %get-tuple-element.194.refs_2_), channel_id=1, source_target_pairs={{0,8},{8,0},{16,24},{24,16},{1,9},{9,1},{17,25},{25,17},{2,10},{10... | collective-permute-start | bytes 589832 | tf_op jit(solution)/shard_map/ppermute | solution.py:416
  457.1 21.2 %collective-permute-start.74 = (bf16[96,1024]{1,0:T(8,128)(2,1)S(1)}, bf16[96,1024]{1,0:T(8,128)(2,1)S(1)}, u32[]{:S(2)}, u32[]{:S(2)}) collective-permute-start(bf16[96,1024]{1,0:T(8,128)(2,1)S(1)} %get-tuple-element.193.refs_1_), channel_id=1, source_target_pairs={{0,16},{8,24},{16,0},{24,8},{1,17},{9,25},{17,1},{25,9},{2,18},{10... | collective-permute-start | bytes 589832 | tf_op jit(solution)/shard_map/ppermute | solution.py:416
  458.5 19.7 %collective-permute-start.76 = (bf16[96,1024]{1,0:T(8,128)(2,1)S(1)}, bf16[96,1024]{1,0:T(8,128)(2,1)S(1)}, u32[]{:S(2)}, u32[]{:S(2)}) collective-permute-start(bf16[96,1024]{1,0:T(8,128)(2,1)S(1)} %copy-done.71), channel_id=1, source_target_pairs={{0,16},{8,24},{16,0},{24,8},{1,17},{9,25},{17,1},{25,9},{2,18},{10... | collective-permute-start | bytes 589832 | tf_op jit(solution)/shard_map/ppermute | solution.py:416
  459.1 19.2 %collective-permute-start.77 = (bf16[96,1024]{1,0:T(8,128)(2,1)S(1)}, bf16[96,1024]{1,0:T(8,128)(2,1)S(1)}, u32[]{:S(2)}, u32[]{:S(2)}) collective-permute-start(bf16[96,1024]{1,0:T(8,128)(2,1)S(1)} %collective-permute-done.75.refs_6_), channel_id=1, source_target_pairs={{0,8},{8,0},{16,24},{24,16},{1,9},{9,1},{17,25},{25,17},{2,10},{10... | collective-permute-start | bytes 589832 | tf_op jit(solution)/shard_map/ppermute | solution.py:416
  (188 other events, 2048.9 us)
Sparse Core Ops, SparseCore 0:
  10.5 67.4 all-gather.1
  498.3 74.9 all-reduce.4

commit v2 on v0

v2 whole, which is shorter than its diff:
```python
import functools
import math

import jax
import jax.numpy as jnp
import numpy as np
from jax import lax
from jax.experimental import pallas as pl
from jax.experimental.pallas import tpu as pltpu
from jax.sharding import PartitionSpec as P

HEADS = 12
LAYERS = 2
STEP = 7
BETA_ONE = 0.9
BETA_TWO = 0.999
LEARN_RATE = 0.1
VECTOR_RATE = 0.5
WEIGHT_DECAY = 0.01
ADAM_EPSILON = 1e-08
NORM_EPSILON = 1e-12
MASK_FILL = -1e30
AUG = 16
QUARTER = 128
LANES = 128
VMEM_LIMIT = 56 * 1024 * 1024
F32 = jnp.float32
BF16 = jnp.bfloat16


def CHUNKS(sequences):
    return [(sequences + 1) // 2, sequences // 2]


def nn(a, b):
    return lax.dot_general(a, b, (((1,), (0,)), ((), ())), preferred_element_type=F32)


def nt(a, b):
    return lax.dot_general(a, b, (((1,), (1,)), ((), ())), preferred_element_type=F32)


def tn(a, b):
    return lax.dot_general(a, b, (((0,), (0,)), ((), ())), preferred_element_type=F32)


def block_layout(groups, layers):
    counts = []
    block_matrix = []
    block_step = []
    for layer_index in range(layers):
        for matrix_type in range(6):
            amount = 1 if matrix_type < 3 else groups
            for position in range(amount):
                block_matrix.append(layer_index * 6 + matrix_type)
                block_step.append(position)
            counts.append(amount)
    return (
        np.array(counts, np.int32),
        np.array(block_matrix, np.int32),
        np.array(block_step, np.int32),
    )


def slot_index(owners, groups, layers, capacity):
    counts, block_matrix, block_step = block_layout(groups, layers)
    matrix_ids = jnp.arange(counts.shape[0], dtype=jnp.int32)
    same_owner = owners[:, None] == owners[None, :]
    earlier = matrix_ids[None, :] < matrix_ids[:, None]
    slot_of = jnp.sum(
        jnp.where(same_owner & earlier, jnp.asarray(counts, jnp.int32)[None, :], 0), axis=1
    )
    starts = owners * capacity + slot_of
    choose = (jnp.asarray(block_matrix, jnp.int32)[:, None] == matrix_ids[None, :]).astype(
        jnp.int32
    )
    return jnp.sum(choose * starts[None, :], axis=1) + jnp.asarray(block_step, jnp.int32)


def pack(square):
    half = square.shape[0] // 2
    return jnp.concatenate([square[:half], square[half:]], axis=1)


def unpack(packed):
    width = packed.shape[1] // 2
    return jnp.concatenate([packed[:, :width], packed[:, width:]], axis=0)


def lanes(value):
    total = value[:, :LANES]
    for at in range(LANES, value.shape[1], LANES):
        total = total + value[:, at : at + LANES]
    return total


def row_totals(value):
    return jnp.sum(lanes(value), axis=1, keepdims=True)


def accumulate(ref, index, value):
    first = pl.program_id(0) == 0

    @pl.when(first)
    def _():
        ref[index] = value

    @pl.when(jnp.logical_not(first))
    def _():
        ref[index] = ref[index] + value


def split3(value):
    high = value.astype(BF16)
    rest = value - high.astype(F32)
    mid = rest.astype(BF16)
    last = (rest - mid.astype(F32)).astype(BF16)
    return high, mid, last


def segment_rows(segs):
    row = lax.broadcasted_iota(jnp.int32, (AUG, segs.shape[1]), 0)
    same = row == segs
    query_rows = jnp.where(same | (row >= 4), 0.0, MASK_FILL)
    key_rows = jnp.where(same | ((row >= 4) & (row < 7)), 1.0, 0.0)
    return query_rows, key_rows.astype(BF16)


def with_rows(query_rows, value):
    high, mid, last = split3(-value)
    row = lax.broadcasted_iota(jnp.int32, query_rows.shape, 0)
    out = jnp.where(row == 4, high.astype(F32), query_rows)
    out = jnp.where(row == 5, mid.astype(F32), out)
    out = jnp.where(row == 6, last.astype(F32), out)
    return out.astype(BF16)


def norm_cdf(u):
    a = jnp.abs(u) * math.sqrt(0.5)
    t = 1.0 / (1.0 + 0.3275911 * a)
    bell = jnp.exp(-a * a)
    poly = t * (
        0.254829592
        + t * (-0.284496736 + t * (1.421413741 + t * (-1.453152027 + t * 1.061405429)))
    )
    tail = (0.5 * poly) * bell
    return jnp.where(u < 0, tail, 1.0 - tail), bell * (1.0 / math.sqrt(2.0 * math.pi))


def attend_body(first, per_group, groups, *refs):
    if first:
        x_ref, seg_ref, w_ref, vec_ref, qkv_ref, ctx_ref, lse_ref, sent = refs
    else:
        pieces, seg_ref, w_ref, vec_ref, x_ref, qkv_ref, ctx_ref, lse_ref, sent = refs
        for j in range(groups):
            x_ref[:, j * QUARTER : (j + 1) * QUARTER] = pieces[j]
    x = x_ref[...]
    width = x.shape[0]
    size = width // per_group
    vec = vec_ref[...]
    q = (nn(w_ref[0], x) + vec[:, 0:1]).astype(BF16)
    k = nn(w_ref[1], x).astype(BF16)
    v = (nn(w_ref[2], x) + vec[:, 1:2]).astype(BF16)
    qkv_ref[0:width] = q
    qkv_ref[width : 2 * width] = k
    qkv_ref[2 * width : 3 * width] = v
    query_rows, key_rows = segment_rows(seg_ref[0])
    query_rows = query_rows.astype(BF16)
    scale = size ** (-0.5)
    length = x.shape[1]
    tile = 256
    for h in range(per_group):
        part = slice(h * size, (h + 1) * size)
        qa = jnp.concatenate([q[part] * jnp.asarray(scale, BF16), query_rows], axis=0)
        ka = jnp.concatenate([k[part], key_rows], axis=0)
        for at in range(0, length, tile):
            cols = slice(at, at + tile)
            s = tn(ka, qa[:, cols])
            top = jnp.max(s, axis=0, keepdims=True)
            e = jnp.exp(s - top)
            total = jnp.sum(e, axis=0, keepdims=True)
            p = (e * (1.0 / total)).astype(BF16)
            ctx_ref[part, cols] = nn(v[part], p).astype(BF16)
            lse_ref[h : h + 1, cols] = top + jnp.log(total)
    for j in range(groups):
        sent[j] = ctx_ref[:, j * QUARTER : (j + 1) * QUARTER]


def attend_back_body(first, per_group, groups, follows, pieces, *refs):
    ctx_ref, qkv_ref, lse_ref, x_ref, seg_ref, w_ref = refs[:6]
    refs = refs[6 + follows :]
    if first:
        dx_ref, gqkv_ref, acc_ref, dctx_ref, gsum_ref, asum_ref = refs
    else:
        out_ref, sent, gqkv_ref, acc_ref, dctx_ref, gsum_ref, asum_ref, dx_ref = refs
    width, length = ctx_ref.shape
    size = width // per_group
    scale = size ** (-0.5)
    for j in range(groups):
        cols = slice(j * QUARTER, (j + 1) * QUARTER)
        dctx_ref[:, cols] = pieces[j, :width]
        if not first:
            out_ref[:, cols] = pieces[j, width:].astype(F32)
    ctx = ctx_ref[...]
    dctx = dctx_ref[...]
    x = x_ref[...]
    query_rows, key_rows = segment_rows(seg_ref[0])
    zero_rows = jnp.zeros_like(query_rows)
    q = qkv_ref[0:width]
    k = qkv_ref[width : 2 * width]
    v = qkv_ref[2 * width : 3 * width]
    dq, dk, dv = [], [], []
    for h in range(per_group):
        part = slice(h * size, (h + 1) * size)
        qh, kh, vh, dch = q[part], k[part], v[part], dctx[part]
        qs = qh * jnp.asarray(scale, BF16)
        delta = jnp.sum(dch.astype(F32) * ctx[part].astype(F32), axis=0, keepdims=True)
        qa = jnp.concatenate([qs, with_rows(query_rows, lse_ref[h : h + 1])], axis=0)
        ka = jnp.concatenate([kh, key_rows], axis=0)
        da = jnp.concatenate([dch, with_rows(zero_rows, delta)], axis=0)
        va = jnp.concatenate([vh, key_rows], axis=0)
        p = jnp.exp(tn(ka, qa))
        ds = (p * tn(va, da)).astype(BF16)
        dv.append(nt(dch, p.astype(BF16)))
        dq.append(nn(kh, ds) * scale)
        dk.append(nt(qs, ds))
    dq = jnp.concatenate(dq, axis=0)
    dk = jnp.concatenate(dk, axis=0)
    dv = jnp.concatenate(dv, axis=0)
    accumulate(asum_ref, 0, lanes(dq))
    accumulate(asum_ref, 1, lanes(dv))
    dx = None
    for at, grad in enumerate((dq, dk, dv)):
        low = grad.astype(BF16)
        accumulate(gsum_ref, at, nt(x, low))
        term = nn(w_ref[at], low)
        dx = term if dx is None else dx + term
    dx_ref[...] = dx
    for j in range(groups):
        cols = slice(j * QUARTER, (j + 1) * QUARTER)
        if first:
            dx_ref[:, cols] = dx_ref[:, cols] + pieces[j, width:].astype(F32)
        else:
            sent[j] = dx_ref[:, cols].astype(BF16)

    @pl.when(pl.program_id(0) == pl.num_programs(0) - 1)
    def _():
        for at in range(3):
            gqkv_ref[at] = pack(gsum_ref[at].astype(BF16))
        acc_ref[...] = jnp.concatenate(
            [jnp.sum(asum_ref[row], axis=1, keepdims=True) for row in range(2)], axis=1
        )


def norm(value):
    centre = jnp.mean(value, axis=0, keepdims=True)
    off = value - centre
    inverse = lax.rsqrt(jnp.mean(off * off, axis=0, keepdims=True) + NORM_EPSILON)
    return off * inverse, inverse


def norm_back(grad, gain, normed, inverse):
    e = grad * gain
    return inverse * (
        e - jnp.mean(e, axis=0, keepdims=True) - normed * jnp.mean(e * normed, axis=0, keepdims=True)
    )


def columns(vec_ref, row):
    return jnp.concatenate([vec_ref[a][:, row : row + 1] for a in range(vec_ref.shape[0])], axis=0)


def layer_forward(x, ctx, w, vec_ref, hid_ref, gp_ref):
    groups, width, nv = vec_ref.shape
    nup = nv - 8
    r1 = x + (nn(w["out_t"][...], ctx) + columns(vec_ref, 2))
    n1, i1 = norm(r1)
    y1 = n1 * columns(vec_ref, 4 + nup) + columns(vec_ref, 5 + nup)
    yl = y1.astype(BF16)
    branch = []
    for a in range(groups):
        own = yl[a * width : (a + 1) * width]
        for j in range(nup):
            rows = slice(j * width, (j + 1) * width)
            u = nn(w["up_t"][a, rows], own) + vec_ref[a][:, 3 + j : 4 + j]
            cdf, bell = norm_cdf(u)
            at = slice((a * nup + j) * width, (a * nup + j + 1) * width)
            hid_ref[at] = (u * cdf).astype(BF16)
            gp_ref[at] = (cdf + u * bell).astype(BF16)
        branch.append(nn(w["down_t"][a], hid_ref[a * nup * width : (a + 1) * nup * width]))
    r2 = y1 + (jnp.concatenate(branch, axis=0) + columns(vec_ref, 3 + nup))
    n2, i2 = norm(r2)
    x2 = n2 * columns(vec_ref, 6 + nup) + columns(vec_ref, 7 + nup)
    return x2, n1, i1, yl, n2, i2


def layer_backward(dy, ctx, w, vec_ref, n1, i1, yl, n2, i2, hid_ref, gp_ref, sums_out):
    put = sums_out.put
    groups, width, nv = vec_ref.shape
    nup = nv - 8
    hidden = nup * width
    sums = [None] * (nv - 2)
    sums[6 + nup - 2 + 0] = row_totals(dy * n2)
    sums[7 + nup - 2 + 0] = row_totals(dy)
    dz = norm_back(dy, columns(vec_ref, 6 + nup), n2, i2)
    sums[3 + nup - 2] = row_totals(dz)
    dzl = dz.astype(BF16)
    sums_out.ready()
    back = []
    bias = [[] for _ in range(nup)]
    for a in range(groups):
        own = slice(a * width, (a + 1) * width)
        total = None
        for j in range(nup):
            at = slice((a * nup + j) * width, (a * nup + j + 1) * width)
            rows = slice(j * width, (j + 1) * width)
            put(a, groups + nup + j, nt(hid_ref[at], dzl[own]))
            du = nn(w["down"][a, rows], dzl[own]) * gp_ref[at].astype(F32)
            bias[j].append(row_totals(du))
            dul = du.astype(BF16)
            put(a, groups + j, nt(yl[own], dul))
            term = nn(w["up"][a, :, rows], dul)
            total = term if total is None else total + term
        back.append(total)
        sums_out.send(a, groups, 2 * nup)
    for j in range(nup):
        sums[3 + j - 2] = jnp.concatenate(bias[j], axis=0)
    dy1 = dz + jnp.concatenate(back, axis=0)
    sums[4 + nup - 2] = row_totals(dy1 * n1)
    sums[5 + nup - 2] = row_totals(dy1)
    dr1 = norm_back(dy1, columns(vec_ref, 4 + nup), n1, i1)
    sums[0] = row_totals(dr1)
    dal = dr1.astype(BF16)
    dctx = nn(w["out"][...], dal).astype(BF16)
    for a in range(groups):
        own = nt(ctx[a * width : (a + 1) * width], dal)
        for b in range(groups):
            put(a, a ^ b, own[:, b * width : (b + 1) * width])
        sums_out.send(a, 0, groups)
    stack = jnp.concatenate(sums, axis=1)
    for a in range(groups):
        flat = jnp.concatenate(
            [stack[a * width : (a + 1) * width], jnp.zeros((width, LANES - len(sums)), F32)], axis=1
        ).T
        flat = flat[: width // 2]
        put(a, groups + 2 * nup, jnp.concatenate([flat, jnp.zeros_like(flat)], axis=1), packed=True)
        sums_out.send(a, groups + 2 * nup, 1)
    return dr1, dctx


WEIGHTS = ("out", "out_t", "up", "up_t", "down", "down_t")


class Fetched:
    def __init__(self, names, sources, places, sems):
        self.places = dict(zip(names, places))
        self.copies = {
            name: pltpu.make_async_copy(source, place, sems.at[at])
            for at, (name, source, place) in enumerate(zip(names, sources, places))
        }
        for copy in self.copies.values():
            copy.start()

    def __getitem__(self, name):
        copy = self.copies.pop(name, None)
        if copy is not None:
            copy.wait()
        return self.places[name]


class Sums:
    def __init__(self, me, core, keep_ref, give_ref, held_ref, before, sems):
        self.me, self.core, self.refs, self.held, self.sems = me, core, (keep_ref, give_ref), held_ref, sems
        self.run = keep_ref.shape[1]
        self.used, self.sent, self.loads, self.before = 0, [], [], before is not None
        if self.before:
            for a in range(held_ref.shape[0]):
                for side in range(2):
                    held = held_ref.at[a, pl.ds(side * self.run, self.run)]
                    self.loads.append(self.either(side, [ref.at[a ^ me] for ref in before], held, False))

    def either(self, side, places, held, out):
        sem = self.sems.at[self.used]
        self.used += 1
        keep, give = (
            pltpu.make_async_copy(held, place, sem) if out else pltpu.make_async_copy(place, held, sem)
            for place in places
        )
        pl.when(self.core == side)(keep.start)
        pl.when(self.core != side)(give.start)
        return keep

    def ready(self):
        for load in self.loads:
            load.wait()

    def put(self, a, j, block, packed=False):
        block = block if packed else pack(block)
        if self.before:
            block = block + self.held[a, j].astype(F32)
        self.held[a, j] = block.astype(BF16)

    def send(self, a, first, count):
        for side in range(2):
            low, high = max(first, side * self.run), min(first + count, (side + 1) * self.run)
            if low < high:
                part = pl.ds(low - side * self.run, high - low)
                places = [ref.at[a ^ self.me, part] for ref in self.refs]
                self.sent.append(self.either(side, places, self.held.at[a, pl.ds(low, high - low)], True))

    def finish(self):
        for copy in self.sent:
            copy.wait()


def joined(me, ref, rows=slice(None), cols=slice(None)):
    return jnp.concatenate([ref[a ^ me, rows, cols] for a in range(ref.shape[0])], axis=0)


def early_body(groups, first, count, me_ref, ctx_ref, x_ref, *refs):
    names = ("out_t", "up_t", "down_t")
    w_refs, vec_ref, sent = refs[:3], refs[3], refs[4]
    x2_ref, n1_ref, n2_ref, inv_ref, hid_ref, gp_ref = refs[5:11]
    w = Fetched(names, w_refs, refs[11:14], refs[14])
    me, width = me_ref[0], vec_ref.shape[1]
    start = joined(me, x_ref, cols=slice(first, first + count)).astype(F32)
    x2, n1, i1, _, n2, i2 = layer_forward(start, joined(me, ctx_ref), w, vec_ref, hid_ref, gp_ref)
    x2_ref[...] = x2
    for a in range(groups):
        sent[a ^ me] = x2[a * width : (a + 1) * width].astype(BF16)
    n1_ref[...] = n1.astype(BF16)
    n2_ref[...] = n2.astype(BF16)
    inv_ref[...] = jnp.concatenate([i1, i2], axis=0)


def middle_body(groups, first, count, follows, me_ref, core_ref, ctx_ref, cot_ref, x_ref, *refs):
    names = ("out_t", "up_t", "down_t", "down", "up", "out")
    w_refs, vec_ref, refs = refs[:6], refs[6], refs[7:]
    before = None
    if follows:
        before, refs = refs[:2], refs[2:]
    sent, dr_ref, keep_ref, give_ref, hid_ref, gp_ref, held_ref, grad_sems = refs[:8]
    w = Fetched(names, w_refs, refs[8:14], refs[14])
    me, width = me_ref[0], vec_ref.shape[1]
    sums_out = Sums(me, core_ref[0], keep_ref, give_ref, held_ref, before, grad_sems)
    ctx = joined(me, ctx_ref)
    x2, n1, i1, yl, n2, i2 = layer_forward(x_ref[...], ctx, w, vec_ref, hid_ref, gp_ref)
    for a in range(groups):
        sent[a ^ me, width:] = x2[a * width : (a + 1) * width].astype(BF16)
    dy = joined(me, cot_ref, cols=slice(first, first + count)).astype(F32)
    dr1, dctx = layer_backward(dy, ctx, w, vec_ref, n1, i1, yl, n2, i2, hid_ref, gp_ref, sums_out)
    dr_ref[...] = dr1
    for a in range(groups):
        sent[a ^ me, :width] = dctx[a * width : (a + 1) * width]
    sums_out.finish()


def late_body(groups, follows, me_ref, core_ref, got_ref, ctx_ref, *refs):
    names = ("down", "up", "out")
    dr_ref, n1_ref, n2_ref, inv_ref, hid_ref, gp_ref = refs[:6]
    w_refs, vec_ref, refs = refs[6:9], refs[9], refs[10:]
    before = None
    if follows:
        before, refs = refs[:2], refs[2:]
    sent, keep_ref, give_ref, held_ref, grad_sems = refs[:5]
    w = Fetched(names, w_refs, refs[5:8], refs[8])
    me, width = me_ref[0], vec_ref.shape[1]
    sums_out = Sums(me, core_ref[0], keep_ref, give_ref, held_ref, before, grad_sems)
    nup = vec_ref.shape[2] - 8
    dy = dr_ref[...] + joined(me, got_ref).astype(F32)
    n1, n2 = n1_ref[...].astype(F32), n2_ref[...].astype(F32)
    yl = (n1 * columns(vec_ref, 4 + nup) + columns(vec_ref, 5 + nup)).astype(BF16)
    inv = inv_ref[...]
    dr1, dctx = layer_backward(
        dy, joined(me, ctx_ref), w, vec_ref, n1, inv[0:1], yl, n2, inv[1:2], hid_ref, gp_ref, sums_out
    )
    for a in range(groups):
        sent[a ^ me, :width] = dctx[a * width : (a + 1) * width]
        sent[a ^ me, width:] = dr1[a * width : (a + 1) * width].astype(BF16)
    sums_out.finish()


def scatter_body(groups, *refs):
    for source, out in zip(refs[: len(refs) // 2], refs[len(refs) // 2 :]):
        for j in range(groups):
            out[j] = source[:, j * QUARTER : (j + 1) * QUARTER].astype(BF16)


def scatter_quarters(arrays, groups):
    width, tokens = arrays[0].shape
    length = QUARTER * groups
    count = tokens // length
    return pl.pallas_call(
        functools.partial(scatter_body, groups),
        grid=(count,),
        in_specs=[pl.BlockSpec((width, length), lambda i: (0, i))] * len(arrays),
        out_specs=[pl.BlockSpec((groups, width, QUARTER), lambda i: (0, 0, i))] * len(arrays),
        out_shape=[jax.ShapeDtypeStruct((groups, width, QUARTER * count), BF16)] * len(arrays),
        name="scatter_quarters",
    )(*arrays)


def pick_body(plain, turned, ids_ref, source, *refs):
    held, sems = refs[-2], refs[-1]
    count = held.shape[0]
    copies = []
    for at in range(count):
        copies.append(pltpu.make_async_copy(source.at[ids_ref[at]], held.at[at], sems.at[at]))
        copies[-1].start()
    for at in range(count):
        copies[at].wait()
        if plain:
            for copy in range(plain):
                refs[0][copy, at] = held[at]
        else:
            block = unpack(held[at])
            refs[0][at] = block
            if turned:
                refs[1][at] = block.T


def pick(ids, source, plain=0, turned=False):
    count = ids.shape[0]
    half, double = source.shape[1:]
    shape = (plain, count, half, double) if plain else (count, double // 2, double // 2)
    outs = 2 if turned else 1
    res = pl.pallas_call(
        functools.partial(pick_body, plain, turned),
        grid_spec=pltpu.PrefetchScalarGridSpec(
            num_scalar_prefetch=1,
            grid=(1,),
            in_specs=[pl.BlockSpec(memory_space=pltpu.HBM)],
            out_specs=[pl.BlockSpec(shape, lambda i, ids: (0,) * len(shape))] * outs,
            scratch_shapes=[pltpu.VMEM((count, half, double), BF16), pltpu.SemaphoreType.DMA((count,))],
        ),
        out_shape=[jax.ShapeDtypeStruct(shape, BF16)] * outs,
        name="pick",
    )(ids, source)
    return res if turned else res[0]


def arrange_body(groups, nup, core_ref, me_ref, *refs):
    w = dict(zip(WEIGHTS, refs[-6:]))
    got, other = refs[0], refs[1] if len(refs) == 8 else None
    me = me_ref[0]
    share = got.shape[1]
    width = got.shape[3] // 2
    even = core_ref[0] == 0

    def block(a, j):
        if other is None:
            return unpack(got[a ^ me, j])
        near, far = got[a ^ me, j % share], other[a ^ me, j % share]
        return unpack(jnp.where(even, near, far) if j < share else jnp.where(even, far, near))

    for a in range(groups):
        rows = slice(a * width, (a + 1) * width)
        line = [block(a, a ^ b) for b in range(groups)]
        w["out"][rows] = jnp.concatenate(line, axis=1)
        ups = [block(a, groups + j) for j in range(nup)]
        w["up"][a] = jnp.concatenate(ups, axis=1)
        w["up_t"][a] = jnp.concatenate([up.T for up in ups], axis=0)
        downs = [block(a, groups + nup + j) for j in range(nup)]
        w["down"][a] = jnp.concatenate(downs, axis=0)
        w["down_t"][a] = jnp.concatenate([down.T for down in downs], axis=1)
    for b in range(groups):
        w["out_t"][b * width : (b + 1) * width] = jnp.concatenate(
            [block(a, a ^ b).T for a in range(groups)], axis=1
        )


def collect_body(edges, ids_ref, *refs):
    out_ref = refs[-1]
    at = ids_ref[pl.program_id(0)]
    low = 0
    out_ref[...] = jnp.zeros_like(out_ref)
    for ref, high in zip(refs[:-1], edges):

        @pl.when((at >= low) & (at < high))
        def _(ref=ref):
            out_ref[0] = unpack(ref[0]).astype(F32)

        low = high


def collect(places, sources, width):
    specs, edges, low = [], [], 0
    for source in sources:
        count, size = source.shape[0], source.shape[1:]

        def index(i, ids, low=low, count=count):
            return (jnp.clip(ids[i] - low, 0, count - 1), 0, 0)

        specs.append(pl.BlockSpec((1, *size), index))
        low += count
        edges.append(low)
    slots = places.shape[0]
    return pl.pallas_call(
        functools.partial(collect_body, tuple(edges)),
        grid_spec=pltpu.PrefetchScalarGridSpec(
            num_scalar_prefetch=1,
            grid=(slots,),
            in_specs=specs,
            out_specs=pl.BlockSpec((1, width, width), lambda i, ids: (i, 0, 0)),
        ),
        out_shape=table(slots, width, width),
        name="collect",
    )(places, *sources)


def table(*shape):
    return jax.ShapeDtypeStruct(shape, F32)


class Line:
    token = None


HBM_SPEC = pl.BlockSpec(memory_space=pltpu.HBM)


def call(body, name, operands, outs, scalars=(), grid=None, specs=None, out_specs=None, scratch=(), aliases=None,
         flops=0, after=(), far=(), far_outs=()):
    behind = [array for array in (Line.token, *after) if array is not None]
    skip, ahead = len(behind), len(scalars)
    plain, made = body, len(outs)
    inputs = len(operands)
    whole = pl.BlockSpec(memory_space=pltpu.VMEM)

    def body(*refs):
        first, refs = refs[:ahead], refs[ahead + skip :]
        ins, results, rest = refs[:inputs], refs[inputs : inputs + made], refs[inputs + made + 1 :]
        refs[inputs + made][...] = jnp.zeros((8, LANES), F32)
        plain(*first, *ins, *results, *rest)

    any_spec = pl.BlockSpec(memory_space=pl.ANY)
    moved = sum(math.prod(array.shape) * array.dtype.itemsize for array in (*operands, *outs))
    common = dict(
        out_shape=[*outs, table(8, LANES)],
        name=name,
        input_output_aliases={at + ahead + skip: to for at, to in (aliases or {}).items()},
        compiler_params=pltpu.CompilerParams(vmem_limit_bytes=VMEM_LIMIT),
        cost_estimate=pl.CostEstimate(flops=int(flops), bytes_accessed=int(moved), transcendentals=0),
    )
    if grid is None:
        smem = pl.BlockSpec(memory_space=pltpu.SMEM)
        res = pl.pallas_call(
            body,
            in_specs=[smem] * ahead + [any_spec] * skip
            + [HBM_SPEC if at in far else whole for at in range(inputs)],
            out_specs=[HBM_SPEC if at in far_outs else whole for at in range(made)] + [whole],
            scratch_shapes=list(scratch),
            **common,
        )(*scalars, *behind, *operands)
    else:
        res = pl.pallas_call(
            body,
            grid_spec=pltpu.PrefetchScalarGridSpec(
                num_scalar_prefetch=ahead,
                grid=grid,
                in_specs=[any_spec] * skip + list(specs),
                out_specs=list(out_specs) + [pl.BlockSpec((8, LANES), lambda i, *s: (0, 0))],
                scratch_shapes=list(scratch),
            ),
            **common,
        )(*scalars, *behind, *operands)
    Line.token = res[-1]
    return list(res[:-1])


def peer(value, step, axis="grp"):
    count = lax.axis_size(axis)
    return lax.ppermute(value, axis, [(i, i ^ step) for i in range(count)])


def swap(parts, after=None):
    if after is not None:
        parts, _ = lax.optimization_barrier((parts, after))
    return lax.all_to_all(parts, "grp", split_axis=0, concat_axis=0)


def adam_step(param, grad, first, second, decay, rate):
    first_new = BETA_ONE * first + (1.0 - BETA_ONE) * grad
    second_new = BETA_TWO * second + (1.0 - BETA_TWO) * grad * grad
    first_hat = first_new / (1.0 - BETA_ONE**STEP)
    second_hat = second_new / (1.0 - BETA_TWO**STEP)
    updated = param - rate * (first_hat / (jnp.sqrt(second_hat) + ADAM_EPSILON) + decay * param)
    return (updated, first_new, second_new)


def shards(
    tokens,
    segments,
    owners,
    masters,
    first_moment,
    second_moment,
    vectors,
    vector_first,
    vector_second,
    cotangent,
):
    groups = lax.axis_size("grp")
    me = lax.axis_index("grp").astype(jnp.int32)
    own_row = lax.axis_index("row").astype(jnp.int32)
    core = lax.rem(own_row, 2)
    capacity = masters.shape[1]
    width, tokens_here = tokens.shape
    half = width // 2
    fg = groups * width
    sequences, length = segments.shape
    per_group = HEADS // groups
    nv = vectors.shape[1]
    nup = nv - 8
    per_layer = 3 + 3 * groups
    segs = segments.reshape(sequences, 1, length)
    order = jnp.arange(groups, dtype=jnp.int32) ^ me
    here, core_at = me.reshape(1), core.reshape(1)
    square = width * width

    block_index = slot_index(owners, groups, LAYERS, capacity)
    ids = block_index.reshape(LAYERS, per_layer)
    relative = jnp.take(ids[:, 3 : 3 + groups], order, axis=1, mode="clip")
    ids = jnp.concatenate([ids[:, :3], relative, ids[:, 3 + groups :]], axis=1)
    local_blocks = masters[0].astype(BF16).reshape(capacity, 2, half, width)
    local_blocks = jnp.concatenate([local_blocks[:, 0], local_blocks[:, 1]], axis=2)
    everyone = lax.all_gather(local_blocks, "row", axis=0, tiled=True)

    x_parts, cot_parts = (swap(part) for part in scatter_quarters([tokens, cotangent], groups))
    vec_all = jnp.stack([vectors] + [peer(vectors, k) for k in range(1, groups)]).transpose(1, 0, 3, 2)
    vecs = [vec_all[l] for l in range(LAYERS)]
    own_vecs = [vec_all[l, 0] for l in range(LAYERS)]

    share = (3 * groups) // 2
    w_qkv, w_turned, dense, exchanged = [None] * LAYERS, [None] * LAYERS, [None] * LAYERS, [None] * LAYERS

    def fetch(l, after=None):
        source, _ = lax.optimization_barrier((everyone, (vec_all, x_parts, cot_parts) if after is None else after))
        mine = ids[l, 3:] if l else lax.dynamic_slice(ids[l], (3 + core * share,), (share,))
        send = pick(mine, source, plain=1 if l else groups)
        w_qkv[l], w_turned[l] = pick(ids[l, :3], source, turned=True)
        if l == 0:
            exchanged[l] = swap(send)
        else:
            exchanged[l] = lax.all_gather(send[0], "grp", axis=0)

    def arrange(l):
        got = [exchanged[l]]
        if l == 0:
            got.append(peer(got[0], 1, "row"))
        shapes = [(fg, fg), (fg, fg), (groups, width, fg), (groups, fg, width), (groups, fg, width), (groups, width, fg)]
        smem, vmem = pl.BlockSpec(memory_space=pltpu.SMEM), pl.BlockSpec(memory_space=pltpu.VMEM)
        res = pl.pallas_call(
            functools.partial(arrange_body, groups, nup),
            in_specs=[smem, smem] + [vmem] * len(got),
            out_specs=[vmem] * 6,
            out_shape=[jax.ShapeDtypeStruct(shape, BF16) for shape in shapes],
            name="arrange",
            compiler_params=pltpu.CompilerParams(vmem_limit_bytes=VMEM_LIMIT),
        )(core_at, here, *got)
        dense[l] = dict(zip(WEIGHTS, res))

    def weight_places(names):
        shapes = {"out": (fg, fg), "up": (groups, width, fg), "down": (groups, fg, width)}
        shapes |= {"out_t": (fg, fg), "up_t": (groups, fg, width), "down_t": (groups, width, fg)}
        return [pltpu.VMEM(shapes[name], BF16) for name in names] + [pltpu.SemaphoreType.DMA((len(names),))]

    fetch(0)

    chunks, at = [], 0
    for count in CHUNKS(sequences):
        chunks.append((at, count))
        at += count
    keep = [dict() for _ in chunks]
    state = {"out": None, "grad": None}
    Line.token = None

    def tok(rows):
        return pl.BlockSpec((rows, length), lambda i, *s: (0, i))

    def quart(rows=width):
        return pl.BlockSpec((groups, rows, QUARTER), lambda i, *s: (0, 0, i))

    def parts(count, rows=width):
        return jax.ShapeDtypeStruct((groups, rows, count * QUARTER), BF16)

    def whole(*shape):
        return pl.BlockSpec(shape, lambda i, *s: (0,) * len(shape))

    def sent(c, key):
        return keep[c - 1][key] if c else None

    def attend(c, l):
        first, count = chunks[c]
        kp = keep[c]
        here_tokens = count * length
        shifted = pl.BlockSpec((width, length), lambda i, *s: (0, i + first))
        seg_spec = pl.BlockSpec((1, 1, length), lambda i, *s: (i + first, 0, 0))
        operands = [segs, w_turned[l], own_vecs[l]]
        specs = [seg_spec, whole(3, width, width), whole(width, nv)]
        outs = [jax.ShapeDtypeStruct((3 * width, here_tokens), BF16), jax.ShapeDtypeStruct((width, here_tokens), BF16),
                table(per_group, here_tokens)]
        out_specs = [tok(3 * width), tok(width), tok(per_group)]
        outs.append(parts(count))
        out_specs.append(quart())
        if l == 0:
            operands, specs = [tokens] + operands, [shifted] + specs
        else:
            operands, specs = [kp["x", l]] + operands, [quart()] + specs
            outs = [jax.ShapeDtypeStruct((width, here_tokens), BF16)] + outs
            out_specs = [tok(width)] + out_specs
        res = call(
            functools.partial(attend_body, l == 0, per_group, groups), "attend", operands, outs, (),
            (count,), specs, out_specs, flops=here_tokens * (6 * square + 4 * width * length),
        )
        if l:
            kp["xl", l] = res.pop(0)
        kp["qkv", l], kp["ctx", l], kp["lse", l] = res[:3]
        if l:
            kp["far", l] = swap(res[3], sent(c, ("far", l)))
        else:
            kp["parts"] = res[3]

    def early(c, l):
        first, count = chunks[c]
        kp = keep[c]
        n = count * QUARTER
        names = ("out_t", "up_t", "down_t")
        outs = [parts(count), table(fg, n), jax.ShapeDtypeStruct((fg, n), BF16), jax.ShapeDtypeStruct((fg, n), BF16),
                                 table(2, n), jax.ShapeDtypeStruct((groups * nup * width, n), BF16),
                                 jax.ShapeDtypeStruct((groups * nup * width, n), BF16)]
        res = call(
            functools.partial(early_body, groups, first * QUARTER, n), "early",
            [kp["far", l], x_parts, *(dense[l][name] for name in names), vecs[l]], outs, [here],
            scratch=weight_places(names), far=range(2, 5), after=[keep[-1]["far", 0]] if c == 0 else (),
            flops=2 * n * groups * square * (groups + 2 * nup),
        )
        kp["x", l + 1] = swap(res[0], sent(c, ("x", l + 1)))
        kp["res", l] = res[1]
        kp["kept", l] = res[2:]

    def grads_before(c, key):
        return [] if c == 0 else list(keep[c - 1][key])

    side_run = (3 * groups + 2) // 2
    stash = jax.ShapeDtypeStruct((groups, side_run, half, 2 * width), BF16)
    stash_places = [
        pltpu.VMEM((groups, 2 * side_run, half, 2 * width), BF16),
        pltpu.SemaphoreType.DMA((8 * groups,)),
    ]

    def middle(c, l):
        first, count = chunks[c]
        kp = keep[c]
        n = count * QUARTER
        before = grads_before(c, ("grads", l))
        hidden = pltpu.VMEM((groups * nup * width, n), BF16)
        names = ("out_t", "up_t", "down_t", "down", "up", "out")
        w_at = 3
        res = call(
            functools.partial(middle_body, groups, first * QUARTER, n, bool(before)), "middle",
            [kp["far", l], cot_parts, kp["res", l - 1], *(dense[l][name] for name in names), vecs[l], *before],
            [parts(count, 2 * width), table(fg, n), stash, stash], [here, core_at],
            scratch=[hidden, hidden, *stash_places, *weight_places(names)],
            far=[*range(w_at, w_at + 6), w_at + 7, w_at + 8], far_outs=[2, 3],
            flops=6 * n * groups * square * (groups + 2 * nup),
        )
        kp["dctx", l] = swap(res[0], sent(c, ("dctx", l)))
        kp["dr", l], kp["grads", l] = res[1], res[2:]

    def late(c, l):
        first, count = chunks[c]
        kp = keep[c]
        n = count * QUARTER
        before = grads_before(c, ("grads", l))
        names = ("down", "up", "out")
        w_at = 8
        res = call(
            functools.partial(late_body, groups, bool(before)), "late",
            [kp["dx", l + 1], kp["far", l], kp["dr", l + 1], *kp["kept", l],
             *(dense[l][name] for name in names), vecs[l], *before],
            [parts(count, 2 * width), stash, stash], [here, core_at],
            scratch=[*stash_places, *weight_places(names)],
            far=[*range(w_at, w_at + 3), w_at + 4, w_at + 5], far_outs=[1, 2],
            flops=4 * n * groups * square * (groups + 2 * nup),
        )
        kp["dctx", l] = swap(res[0], sent(c, ("dctx", l)))
        kp["grads", l] = res[1:]

    def attend_back(c, l):
        first, count = chunks[c]
        kp = keep[c]
        here_tokens = count * length
        shifted = pl.BlockSpec((width, length), lambda i, *s: (0, i + first))
        seg_spec = pl.BlockSpec((1, 1, length), lambda i, *s: (i + first, 0, 0))
        operands = [kp["dctx", l], kp["ctx", l], kp["qkv", l], kp["lse", l], tokens if l == 0 else kp["xl", l], segs,
                    w_qkv[l]]
        specs = [quart(2 * width), tok(width), tok(3 * width), tok(per_group), shifted if l == 0 else tok(width),
                                      seg_spec, whole(3, width, width)]
        outs = [jax.ShapeDtypeStruct((3, half, 2 * width), BF16), table(width, 2)]
        out_specs = [whole(3, half, 2 * width), whole(width, 2)]
        scratch = [pltpu.VMEM((width, length), BF16), pltpu.VMEM((3, width, width), F32),
                   pltpu.VMEM((2, width, LANES), F32)]
        name = "grad" if l == 0 else "out"
        aliases, follows = None, state[name] is not None
        if follows:
            aliases = {len(operands): 0}
            operands.append(state[name])
            specs.append(pl.BlockSpec(memory_space=pl.ANY))
        if l:
            outs = [parts(count)] + outs
            out_specs = [quart()] + out_specs
            scratch.append(pltpu.VMEM((width, length), F32))
        res = call(
            functools.partial(attend_back_body, l == 0, per_group, groups, follows), "attend_back", operands,
            [table(width, tokens_here)] + outs, (), (count,), specs, [shifted] + out_specs, scratch, aliases,
            here_tokens * (12 * square + 10 * width * length),
            after=[gate] if l == 0 and follows else (),
        )
        state[name] = res[0]
        if l:
            kp["dx", l] = swap(res[1], sent(c, ("dx", l)))
        kp["gqkv", l], kp["gvec", l] = res[-2:]

    def both(key, l):
        return sum(kp[key, l].astype(F32) for kp in keep)

    def scattered(l):
        kept, give = keep[-1]["grads", l]
        give, _ = lax.optimization_barrier((give, keep[0]["dctx", l]))
        got = peer(give, 1, "row")
        if l:
            return lax.psum_scatter(kept + got, "grp", scatter_dimension=0)

        def part(k):
            return lax.dynamic_index_in_dim(kept, me ^ k, 0, False) + lax.dynamic_index_in_dim(got, me ^ k, 0, False)

        return sum(peer(part(k), k).astype(F32) if k else part(k).astype(F32) for k in range(groups)).astype(BF16)

    def side_blocks(l, after=None):
        rows = jnp.pad(both("gvec", l).T, ((0, half - 2), (0, width)))
        all_four = jnp.concatenate([both("gqkv", l), rows[None]], axis=0).astype(BF16)
        if after is not None:
            all_four, _ = lax.optimization_barrier((all_four, after))
        mine = lax.dynamic_slice_in_dim(all_four, 2 * core, 2)
        return mine + peer(lax.dynamic_slice_in_dim(all_four, 2 - 2 * core, 2), 1, "row")

    class ChipSum:
        def __init__(self, value):
            self.shape = value.shape
            self.flat = value.reshape(-1, 2 * width)
            self.rows = self.flat.shape[0] // 2
            self.high = lax.rem(own_row // 2, 2)

        def first(self, after=None):
            give = lax.dynamic_slice_in_dim(self.flat, (1 - self.high) * self.rows, self.rows)
            if after is not None:
                give, _ = lax.optimization_barrier((give, after))
            got = peer(give, 2, "row")
            self.mine = lax.dynamic_slice_in_dim(self.flat, self.high * self.rows, self.rows) + got
            return got

        def second(self, after=None):
            got, step = None, 4
            while step < lax.axis_size("row"):
                give = self.mine
                if after is not None:
                    give, _ = lax.optimization_barrier((give, after))
                got = peer(give, step, "row")
                self.mine = self.mine + got
                step *= 2
            return got

        def third(self):
            return peer(self.mine, 2, "row")

        def whole(self, other):
            first = self.high == 0
            parts = [jnp.where(first, self.mine, other), jnp.where(first, other, self.mine)]
            return jnp.concatenate(parts, axis=0).reshape(self.shape)

        def all(self, after=None):
            self.first(after)
            self.second()
            return self.whole(self.third())

    assert LAYERS == 2
    count = len(chunks)
    ends = [None] * LAYERS

    def run(f, l):
        for c in range(count):
            f(c, l)

    run(attend, 0)
    ahead = (exchanged[0], Line.token)
    for kp in keep:
        kp["far", 0] = ahead = swap(kp["parts"], ahead)
    arrange(0)
    run(early, 0)
    fetch(1, keep[-1]["far", 0])
    run(attend, 1)
    arrange(1)
    run(middle, 1)
    run(attend_back, 1)
    chips = ChipSum(jnp.concatenate([scattered(1), side_blocks(1)], axis=0))
    run(late, 0)
    gate = chips.first(keep[0]["dctx", 0])
    big = ChipSum(scattered(0)).all()
    run(attend_back, 0)
    second = chips.second()
    third = chips.third()
    total = chips.whole(third)
    ends[1] = [total, peer(total, 1, "row")]
    total = jnp.concatenate([big, ChipSum(side_blocks(0, second)).all()], axis=0)
    ends[0] = [total, peer(total, 1, "row")]
    sources = ends[0] + ends[1]

    span = side_run + 2

    def places_of(side, at):
        return jnp.where(side == core, 0, span) + at

    j, i = jnp.arange(3 * groups, dtype=jnp.int32), jnp.arange(3, dtype=jnp.int32)
    one = jnp.concatenate([places_of(i // 2, side_run + i % 2), places_of(j // side_run, j % side_run)])
    places = (jnp.arange(LAYERS, dtype=jnp.int32)[:, None] * (2 * span) + one[None, :]).reshape(-1)
    targets = own_row * capacity + jnp.arange(capacity, dtype=jnp.int32)
    match = ids.reshape(-1)[None, :] == targets[:, None]
    place = jnp.sum(jnp.where(match, places[None, :], 0), axis=1)
    place = jnp.where(jnp.any(match, axis=1), place, 1 << 20).astype(jnp.int32)
    own_grads = collect(place, sources, width).reshape(1, capacity, square)

    def vector_rows(l):
        odd = jnp.where(core == 1, sources[2 * l], sources[2 * l + 1])
        rest = odd[3 * groups - side_run]
        return jnp.concatenate([odd[side_run + 1, :2, :width], rest[: nv - 2, :width]], axis=0).astype(F32)

    summed_vectors = jnp.stack([vector_rows(l) for l in range(LAYERS)], axis=0)
    new_masters, new_first, new_second = adam_step(
        masters, own_grads, first_moment, second_moment, WEIGHT_DECAY, LEARN_RATE
    )
    new_vectors, new_vector_first, new_vector_second = adam_step(
        vectors, summed_vectors, vector_first, vector_second, 0.0, VECTOR_RATE
    )
    return (
        state["out"],
        state["grad"],
        new_masters,
        new_first,
        new_second,
        new_vectors,
        new_vector_first,
        new_vector_second,
    )


def solution(mesh):
    in_specs = (
        P("grp", "row"),
        P("row", None),
        P(),
        P("grp", "row", None),
        P("grp", "row", None),
        P("grp", "row", None),
        P(None, None, "grp"),
        P(None, None, "grp"),
        P(None, None, "grp"),
        P("grp", "row"),
    )
    out_specs = (
        P("grp", "row"),
        P("grp", "row"),
        P("grp", "row", None),
        P("grp", "row", None),
        P("grp", "row", None),
        P(None, None, "grp"),
        P(None, None, "grp"),
        P(None, None, "grp"),
    )
    return jax.shard_map(shards, mesh=mesh, in_specs=in_specs, out_specs=out_specs, check_vma=False)
```

time: 1060 us -> 448 us (0.42)
  matrix products: 285 us -> 0 us
  waiting for transfers between devices: 341 us -> 89.3 us
  Pallas kernels: 0 us -> 210 us
  local copies, waits for them, and re-layouts: 182 us -> 17 us
  blocking collectives: 155 us -> 13.5 us
  starting transfers between devices: 0.46 us -> 74.7 us
  other arithmetic: 62.1 us -> 19.6 us
    dot_general x107 -> x0, matrix products: 285 us -> none  [the longest x2 42 us: layer_forward(): jnp.dot(y_low, w_up, preferred_element_type=jnp.float32)]
    pallas_call x0 -> x22, Pallas kernels: none -> 210 us  [the longest x6 89.2 us: call(): pl.pallas_call(body, in_specs=[smem] * ahead + [any_spec] * skip + [HBM_S...]
    reduce_scatter x2 -> x0, waiting for transfers between devices: 157 us -> none  [layer_forward(): mixed = lax.psum_scatter(out_terms, 'grp', scatter_dimension=1, tiled=True)]
    psum x9 -> x0, blocking collectives: 155 us -> none  [the longest x4 64.4 us: normalize(): lax.psum((jnp.sum(resid, axis=1), jnp.sum(resid * resid, axis=1)), 'grp')]
    all_gather x3 -> x2, waiting for transfers between devices: 115 us -> 15.6 us  [the longest x1 15.6 us: shards(): everyone = lax.all_gather(local_blocks, 'row', axis=0, tiled=True)]
    psum x1 -> x0, waiting for transfers between devices: 68.4 us -> none  [shards(): summed_blocks, summed_vectors = lax.psum((flat_grads, vector_grads), 'row')]
    concatenate x15 -> x2, local copies, waits for them, and re-layouts: 57.8 us -> 0.01 us  [vector_rows(): jnp.concatenate([odd[side_run + 1, :2, :width], rest[:nv - 2, :width]], a...]
    all_to_all x0 -> x14, starting transfers between devices: none -> 57.3 us  [swap(): return lax.all_to_all(parts, 'grp', split_axis=0, concat_axis=0)]
  transfers between devices with their start and end apart: 6 -> 39, of which waited for: 5 -> 17; matrix products, arithmetic and copies ran while one was open for 7% -> 5% of each run, Pallas kernels for 0% -> 45%
where the time goes in v2:
time: 448 us; the launch traced here: 439 us
  Pallas kernels  210 us (47%)
  waiting for transfers between devices  89.3 us (20%)
  starting transfers between devices  74.7 us (17%)
  other arithmetic  19.6 us (4%)
  local copies, waits for them, and re-layouts  17 us (4%)
  between operations  15 us (3%)
  blocking collectives  13.5 us (3%)
    pallas_call x6, Pallas kernels, call(): pl.pallas_call(body, in_specs=[smem] * ahead + [any_spec] * skip + [HBM_S...  89.2 us
    pallas_call x8, Pallas kernels, call(): pl.pallas_call(body, grid_spec=pltpu.PrefetchScalarGridSpec(num_scalar_pr...  83.3 us
    all_to_all x14, starting transfers between devices, swap(): return lax.all_to_all(parts, 'grp', split_axis=0, concat_axis=0)  57.3 us
    ppermute x22, waiting for transfers between devices, peer(): return lax.ppermute(value, axis, [(i, i ^ step) for i in range(count)])  39.3 us
    all_to_all x14, waiting for transfers between devices, swap(): return lax.all_to_all(parts, 'grp', split_axis=0, concat_axis=0)  34.3 us
    ppermute x22, starting transfers between devices, peer(): return lax.ppermute(value, axis, [(i, i ^ step) for i in range(count)])  17.1 us
    pallas_call x2, Pallas kernels, arrange(): pl.pallas_call(functools.partial(arrange_body, groups, nup), in_specs=[sm...  16.7 us
    all_gather x1, waiting for transfers between devices, shards(): everyone = lax.all_gather(local_blocks, 'row', axis=0, tiled=True)  15.6 us
  transfers between devices with their start and end apart: 39, of which 17 were waited for; matrix products, arithmetic and copies ran while one was open for 5% of the time, Pallas kernels for 45%

profile of v2, /device:TPU:0, one launch (start us, length us, event | category | flops | bytes accessed | tf_op | source)
XLA Modules:
  0.0 439.3 jit_solution(5933221214508715805)
XLA Ops:
  10.6 4.7 %scatter_quarters.1 = (bf16[4,192,640]{2,1,0:T(8,128)(2,1)}, bf16[4,192,640]{2,1,0:T(8,128)(2,1)}) custom-call(bf16[192,2560]{1,0:T(8,128)(2,1)} %refs_6_.1, f32[192,2560]{1,0:T(8,128)} %refs_1_.2), custom_call_target="tpu_custom_call" | custom-call | tf_op jit(solution)/shard_map/scatter_quarters/pallas_call | solution.py:493
  15.3 5.3 %all-to-all-start = ((bf16[4,192,640]{2,1,0:T(8,128)(2,1)}), bf16[4,192,640]{2,1,0:T(8,128)(2,1)S(1)}, u32[]{:S(2)}, u32[]{:S(2)}) async-start(bf16[4,192,640]{2,1,0:T(8,128)(2,1)} %get-tuple-element.112), calls=%async_computation | async-start | bytes 1966080 | tf_op jit(solution)/shard_map/all_to_all | solution.py:679
  24.4 9.6 %all-to-all-done.refs_4_.refs_3_ = bf16[4,192,640]{2,1,0:T(8,128)(2,1)S(1)} async-done(((bf16[4,192,640]{2,1,0:T(8,128)(2,1)}), bf16[4,192,640]{2,1,0:T(8,128)(2,1)S(1)}, u32[]{:S(2)}, u32[]{:S(2)}) %all-to-all-start) | async-done | bytes 983072 | tf_op jit(solution)/shard_map/all_to_all | solution.py:679
  40.0 9.5 %all-to-all-done.1.refs_4_ = bf16[4,192,640]{2,1,0:T(8,128)(2,1)S(1)} async-done(((bf16[4,192,640]{2,1,0:T(8,128)(2,1)}), bf16[4,192,640]{2,1,0:T(8,128)(2,1)S(1)}, u32[]{:S(2)}, u32[]{:S(2)}) %all-to-all-start.1) | async-done | bytes 983072 | tf_op jit(solution)/shard_map/all_to_all | solution.py:679
  49.5 15.6 %all-gather.3.cloned.1.call-done.source = bf16[64,96,384]{2,1,0:T(8,128)(2,1)} async-done(((bf16[8,96,384]{2,1,0:T(8,128)(2,1)}), bf16[64,96,384]{2,1,0:T(8,128)(2,1)}) %all-gather.3.cloned.1.call-update) | async-done | bytes 4718608 | tf_op jit(solution)/shard_map/all_gather | solution.py:727
  77.2 11.6 %attend.4 = (bf16[576,1536]{1,0:T(8,128)(2,1)}, bf16[192,1536]{1,0:T(8,128)(2,1)}, f32[3,1536]{1,0:T(4,128)}, bf16[4,192,384]{2,1,0:T(8,128)(2,1)}, f32[8,128]{1,0:T(8,128)}) custom-call(bf16[192,2560]{1,0:T(8,128)(2,1)} %refs_6_.1, s32[5,1,512]{2,1,0:T(1,128)} %reshape.188.refs_1_.refs_2_.refs_6_.refs_7_, ...), custom_call_target="tpu_custom_call" | custom-call | flops 943718400 | bytes 4191232 | tf_op jit(solution)/shard_map/attend/pallas_call | solution.py:656
  88.8 8.4 %attend.5 = (bf16[576,1024]{1,0:T(8,128)(2,1)}, bf16[192,1024]{1,0:T(8,128)(2,1)}, f32[3,1024]{1,0:T(4,128)}, bf16[4,192,256]{2,1,0:T(8,128)(2,1)}, f32[8,128]{1,0:T(8,128)}) custom-call(f32[8,128]{1,0:T(8,128)} %get-tuple-element.116.refs_0_, bf16[192,2560]{1,0:T(8,128)(2,1)} %refs_6_.1, s32[5,1,512]{2,1,0:T(1,128)} %reshape.188.refs_1_.refs_2_.refs_6_.refs_7_, ...), custom_call_target="tpu_custom_call" | custom-call | flops 629145600 | bytes 3202048 | tf_op jit(solution)/shard_map/attend/pallas_call | solution.py:656
  97.3 13.5 %all_to_all.75.refs_3_.refs_4_ = bf16[4,192,384]{2,1,0:T(8,128)(2,1)} all-to-all(bf16[4,192,384]{2,1,0:T(8,128)(2,1)S(1)} %copy-done.22), channel_id=1, replica_groups=mesh['grp'=4,'row'=8] {'grp'}, dimensions={0} | all-to-all | bytes 1179648 | tf_op jit(solution)/shard_map/all_to_all | solution.py:679
  115.1 5.0 %all-to-all-done.4.refs_2_.refs_4_ = bf16[4,192,256]{2,1,0:T(8,128)(2,1)S(1)} async-done(((bf16[4,192,256]{2,1,0:T(8,128)(2,1)}), bf16[4,192,256]{2,1,0:T(8,128)(2,1)S(1)}, u32[]{:S(2)}, u32[]{:S(2)}) %all-to-all-start.4) | async-done | bytes 393248 | tf_op jit(solution)/shard_map/all_to_all | solution.py:679
  128.1 8.4 %arrange.2 = (bf16[768,768]{1,0:T(8,128)(2,1)}, bf16[768,768]{1,0:T(8,128)(2,1)}, bf16[4,192,768]{2,1,0:T(8,128)(2,1)}, bf16[4,768,192]{2,1,0:T(8,128)(2,1)}, bf...) custom-call(s32[1]{0:T(128)} %bitcast.1.core_ref.refs_1_, s32[1]{0:T(128)} %bitcast.me_ref.refs_0_, ...), custom_call_target="tpu_custom_call" | custom-call | tf_op jit(solution)/shard_map/arrange/pallas_call | solution.py:753
  136.4 12.4 %early.2 = (bf16[4,192,384]{2,1,0:T(8,128)(2,1)}, f32[768,384]{1,0:T(8,128)}, bf16[768,384]{1,0:T(8,128)(2,1)}, bf16[768,384]{1,0:T(8,128)(2,1)}, f32[2,384]{1,0...) custom-call(s32[1]{0:T(128)} %bitcast.me_ref.refs_0_, ...), custom_call_target="tpu_custom_call" | custom-call | flops 1358954496 | bytes 12819456 | tf_op jit(solution)/shard_map/early/pallas_call | solution.py:647
  152.6 9.5 %early.3 = (bf16[4,192,256]{2,1,0:T(8,128)(2,1)}, f32[768,256]{1,0:T(8,128)}, bf16[768,256]{1,0:T(8,128)(2,1)}, bf16[768,256]{1,0:T(8,128)(2,1)}, f32[2,256]{1,0...) custom-call(s32[1]{0:T(128)} %bitcast.me_ref.refs_0_, ...), custom_call_target="tpu_custom_call" | custom-call | flops 905969664 | bytes 10065920 | tf_op jit(solution)/shard_map/early/pallas_call | solution.py:647
  162.1 6.6 %all-to-all-done.5.refs_1_ = bf16[4,192,384]{2,1,0:T(8,128)(2,1)S(1)} async-done(((bf16[4,192,384]{2,1,0:T(8,128)(2,1)}), bf16[4,192,384]{2,1,0:T(8,128)(2,1)S(1)}, u32[]{:S(2)}, u32[]{:S(2)}) %all-to-all-start.5) | async-done | bytes 589856 | tf_op jit(solution)/shard_map/all_to_all | solution.py:679
  175.0 11.7 %attend.6 = (bf16[192,1536]{1,0:T(8,128)(2,1)}, bf16[576,1536]{1,0:T(8,128)(2,1)}, bf16[192,1536]{1,0:T(8,128)(2,1)}, f32[3,1536]{1,0:T(4,128)}, bf16[4,192,384]{2,1,0:T(8,128)(2,1)}, /*index=5*/f32[8,128]{1,0:T(8,128)}) custom-call(f32[8,128]{1,0:T(8,128)} %get-tuple-element.126.refs_0_, bf16[4,192,384]{2,1,0:T(8,128)(2,1)} %copy-done.21, ...), custom_call_target="tpu_custom_call" | custom-call | flops 943718400 | bytes 4387840 | tf_op jit(solution)/shard_map/attend/pallas_call | solution.py:656
  190.9 8.4 %attend.7 = (bf16[192,1024]{1,0:T(8,128)(2,1)}, bf16[576,1024]{1,0:T(8,128)(2,1)}, bf16[192,1024]{1,0:T(8,128)(2,1)}, f32[3,1024]{1,0:T(4,128)}, bf16[4,192,256]{2,1,0:T(8,128)(2,1)}, /*index=5*/f32[8,128]{1,0:T(8,128)}) custom-call(f32[8,128]{1,0:T(8,128)} %get-tuple-element.130.refs_0_, bf16[4,192,256]{2,1,0:T(8,128)(2,1)} %copy-done.24, ...), custom_call_target="tpu_custom_call" | custom-call | flops 629145600 | bytes 3005440 | tf_op jit(solution)/shard_map/attend/pallas_call | solution.py:656
  199.3 4.6 %all-to-all-start.8 = ((bf16[4,192,256]{2,1,0:T(8,128)(2,1)}), bf16[4,192,256]{2,1,0:T(8,128)(2,1)S(1)}, u32[]{:S(2)}, u32[]{:S(2)}) async-start(bf16[4,192,256]{2,1,0:T(8,128)(2,1)} %get-tuple-element.144), calls=%async_computation.8 | async-start | bytes 786432 | tf_op jit(solution)/shard_map/all_to_all | solution.py:679
  203.9 8.3 %arrange.3 = (bf16[768,768]{1,0:T(8,128)(2,1)}, bf16[768,768]{1,0:T(8,128)(2,1)}, bf16[4,192,768]{2,1,0:T(8,128)(2,1)}, bf16[4,768,192]{2,1,0:T(8,128)(2,1)}, bf...) custom-call(s32[1]{0:T(128)} %bitcast.1.core_ref.refs_1_, s32[1]{0:T(128)} %bitcast.me_ref.refs_0_, ...), custom_call_target="tpu_custom_call" | custom-call | tf_op jit(solution)/shard_map/arrange/pallas_call | solution.py:753
  212.3 21.5 %middle.2 = (bf16[4,384,384]{2,1,0:T(8,128)(2,1)}, f32[768,384]{1,0:T(8,128)}, bf16[4,7,96,384]{3,2,1,0:T(8,128)(2,1)}, bf16[4,7,96,384]{3,2,1,0:T(8,128)(2,1)}, f32[8,128]{1,0:T(8,128)}) custom-call(s32[1]{0:T(128)} %bitcast.me_ref.refs_0_, s32[1]{0:T(128)} %bitcast.1.core_ref.refs_1_, f32[8,128]{1,0:T(8,128)} %get-tuple-element.133.refs_2_, ...), custom_call_target="tpu_custom_call" | custom-call | flops 4076863488 | bytes 16355328 | tf_op jit(solution)/shard_map/middle/pallas_call | solution.py:647
  238.8 17.1 %middle.3 = (bf16[4,384,256]{2,1,0:T(8,128)(2,1)}, f32[768,256]{1,0:T(8,128)}, bf16[4,7,96,384]{3,2,1,0:T(8,128)(2,1)}, bf16[4,7,96,384]{3,2,1,0:T(8,128)(2,1)}, f32[8,128]{1,0:T(8,128)}) custom-call(s32[1]{0:T(128)} %bitcast.me_ref.refs_0_, s32[1]{0:T(128)} %bitcast.1.core_ref.refs_1_, f32[8,128]{1,0:T(8,128)} %get-tuple-element.142.refs_2_, ...), custom_call_target="tpu_custom_call" | custom-call | flops 2717908992 | bytes 19107840 | tf_op jit(solution)/shard_map/middle/pallas_call | solution.py:647
  256.0 4.4 all-to-all-start.10
  260.4 12.6 %attend_back.4 = (f32[192,2560]{1,0:T(8,128)}, bf16[4,192,384]{2,1,0:T(8,128)(2,1)}, bf16[3,96,384]{2,1,0:T(8,128)(2,1)}, f32[192,2]{1,0:T(8,128)}, f32[8,128]{1,0:T(8,128)}) custom-call(f32[8,128]{1,0:T(8,128)} %get-tuple-element.148.refs_0_, bf16[4,384,384]{2,1,0:T(8,128)(2,1)} %copy-done.17, bf16[192,1536]{1,0:T(8,128)(2,1)} %get-tuple-element.150.refs_2_, ...), custom_call_target="tpu_custom_call" | custom-call | flops 2189426688 | bytes 7157248 | tf_op jit(solution)/shard_map/attend_back/pallas_call | solution.py:656
  280.7 9.3 %attend_back.5 = (f32[192,2560]{1,0:T(8,128)}, bf16[4,192,256]{2,1,0:T(8,128)(2,1)}, bf16[3,96,384]{2,1,0:T(8,128)(2,1)}, f32[192,2]{1,0:T(8,128)}, f32[8,128]{1,0:T(8,128)}) custom-call(f32[8,128]{1,0:T(8,128)} %get-tuple-element.155.refs_0_, bf16[4,384,256]{2,1,0:T(8,128)(2,1)} %copy-done.19, ...), custom_call_target="tpu_custom_call", output_to_operand_aliasing={{0}: (8, {})} | custom-call | flops 1459617792 | bytes 7544320 | tf_op jit(solution)/shard_map/attend_back/pallas_call | solution.py:656
  290.0 4.6 %all-to-all-start.12 = ((bf16[4,192,256]{2,1,0:T(8,128)(2,1)}), bf16[4,192,256]{2,1,0:T(8,128)(2,1)S(1)}, u32[]{:S(2)}, u32[]{:S(2)}) async-start(bf16[4,192,256]{2,1,0:T(8,128)(2,1)} %get-tuple-element.177), calls=%async_computation.12 | async-start | bytes 786432 | tf_op jit(solution)/shard_map/all_to_all | solution.py:679
  294.6 15.0 %late.2 = (bf16[4,384,384]{2,1,0:T(8,128)(2,1)}, bf16[4,7,96,384]{3,2,1,0:T(8,128)(2,1)}, bf16[4,7,96,384]{3,2,1,0:T(8,128)(2,1)}, f32[8,128]{1,0:T(8,128)}) custom-call(s32[1]{0:T(128)} %bitcast.me_ref.refs_0_, s32[1]{0:T(128)} %bitcast.1.core_ref.refs_1_, f32[8,128]{1,0:T(8,128)} %get-tuple-element.164.refs_2_, bf16[4,192,384]{2,1,0:T(8,128)(2,1)} %copy-done.10, ...), custom_call_target="tpu_custom_call" | custom-call | flops 2717908992 | bytes 17144832 | tf_op jit(solution)/shard_map/late/pallas_call | solution.py:647
  310.3 4.2 all-to-all-start.13
  314.6 13.7 %late.3 = (bf16[4,384,256]{2,1,0:T(8,128)(2,1)}, bf16[4,7,96,384]{3,2,1,0:T(8,128)(2,1)}, bf16[4,7,96,384]{3,2,1,0:T(8,128)(2,1)}, f32[8,128]{1,0:T(8,128)}) custom-call(s32[1]{0:T(128)} %bitcast.me_ref.refs_0_, s32[1]{0:T(128)} %bitcast.1.core_ref.refs_1_, f32[8,128]{1,0:T(8,128)} %get-tuple-element.175.refs_2_, bf16[4,192,256]{2,1,0:T(8,128)(2,1)} %copy-done.13, ...), custom_call_target="tpu_custom_call" | custom-call | flops 1811939328 | bytes 18126848 | tf_op jit(solution)/shard_map/late/pallas_call | solution.py:647
  346.1 12.2 %attend_back.6 = (f32[192,2560]{1,0:T(8,128)}, bf16[3,96,384]{2,1,0:T(8,128)(2,1)}, f32[192,2]{1,0:T(8,128)}, f32[8,128]{1,0:T(8,128)}) custom-call(f32[8,128]{1,0:T(8,128)} %get-tuple-element.186.refs_0_, bf16[4,384,384]{2,1,0:T(8,128)(2,1)} %copy-done.16, bf16[192,1536]{1,0:T(8,128)(2,1)} %get-tuple-element.188.refs_2_, ...), custom_call_target="tpu_custom_call" | custom-call | flops 2189426688 | bytes 6960640 | tf_op jit(solution)/shard_map/attend_back/pallas_call | solution.py:656
  361.1 4.6 %collective-permute-done.8 = bf16[7,96,384]{2,1,0:T(8,128)(2,1)} collective-permute-done((bf16[7,96,384]{2,1,0:T(8,128)(2,1)}, bf16[7,96,384]{2,1,0:T(8,128)(2,1)}, u32[]{:S(2)}, u32[]{:S(2)}) %collective-permute-start.8) | collective-permute-done | bytes 516128 | tf_op jit(solution)/shard_map/ppermute | solution.py:673
  374.2 9.0 %attend_back.7 = (f32[192,2560]{1,0:T(8,128)}, bf16[3,96,384]{2,1,0:T(8,128)(2,1)}, f32[192,2]{1,0:T(8,128)}, f32[8,128]{1,0:T(8,128)}) custom-call(f32[8,128]{1,0:T(8,128)} %get-tuple-element.192.refs_0_, bf16[432,384]{1,0:T(8,128)(2,1)} %copy-done.15, bf16[4,384,256]{2,1,0:T(8,128)(2,1)} %copy-done.6, ...), custom_call_target="tpu_custom_call", output_to_operand_aliasing={{0}: (9, {})} | custom-call | flops 1459617792 | bytes 7740928 | tf_op jit(solution)/shard_map/attend_back/pallas_call | solution.py:656
  391.2 11.2 %collective-permute-done.12 = bf16[336,384]{1,0:T(8,128)(2,1)S(1)} collective-permute-done((bf16[336,384]{1,0:T(8,128)(2,1)S(1)}, bf16[336,384]{1,0:T(8,128)(2,1)S(1)}, u32[]{:S(2)}, u32[]{:S(2)}) %collective-permute-start.12) | collective-permute-done | bytes 258080 | tf_op jit(solution)/shard_map/ppermute | solution.py:673
  406.6 6.0 %collective-permute-done.13 = bf16[336,384]{1,0:T(8,128)(2,1)S(1)} collective-permute-done((bf16[336,384]{1,0:T(8,128)(2,1)S(1)}, bf16[336,384]{1,0:T(8,128)(2,1)S(1)}, u32[]{:S(2)}, u32[]{:S(2)}) %collective-permute-start.13) | collective-permute-done | bytes 258080 | tf_op jit(solution)/shard_map/ppermute | solution.py:673
  422.0 4.7 %collect.1 = f32[8,192,192]{2,1,0:T(8,128)} custom-call(s32[8]{0:T(128)} %broadcast_select_fusion.8.ids_ref, bf16[9,96,384]{2,1,0:T(8,128)(2,1)} %copy-done.8, bf16[9,96,384]{2,1,0:T(8,128)(2,1)} %copy-done.9, bf16[9,96,384]{2,1,0:T(8,128)(2,1)} %bitcast.69, bf16[9,96,384]{2,1,0:T(8,128)(2,1)} %copy-done.7), custom_call_target="tpu_custom_call" | custom-call | tf_op jit(solution)/shard_map/collect/pallas_call | solution.py:598
  (238 shorter events, 120.9 us)
Async XLA Ops:
  7.2 58.0 %all-gather.3.cloned.1.call-start = ((), (), s32[]{:S(2)}) async-start(), calls=%async_computation.16 | async-start | bytes 5308416 | tf_op jit(solution)/shard_map/all_gather | solution.py:727
  15.3 18.8 %all-to-all-start = ((bf16[4,192,640]{2,1,0:T(8,128)(2,1)}), bf16[4,192,640]{2,1,0:T(8,128)(2,1)S(1)}, u32[]{:S(2)}, u32[]{:S(2)}) async-start(bf16[4,192,640]{2,1,0:T(8,128)(2,1)} %get-tuple-element.112), calls=%async_computation | async-start | bytes 1966080 | tf_op jit(solution)/shard_map/all_to_all | solution.py:679
  20.6 18.9 %collective-permute-start = (f32[2,12,192]{2,0,1:T(2,128)S(1)}, f32[2,12,192]{2,0,1:T(2,128)S(1)}, u32[]{:S(2)}, u32[]{:S(2)}) collective-permute-start(f32[2,12,192]{2,0,1:T(2,128)S(1)} %copy-done.28), channel_id=1, source_target_pairs={{0,8},{8,0},{16,24},{24,16},{1,9},{9,1},{17,25},{25,17},{2,10},{10... | collective-permute-start | bytes 55304 | tf_op jit(solution)/shard_map/ppermute | solution.py:673
  22.7 17.0 %collective-permute-start.1 = (f32[2,12,192]{2,0,1:T(2,128)S(1)}, f32[2,12,192]{2,0,1:T(2,128)S(1)}, u32[]{:S(2)}, u32[]{:S(2)}) collective-permute-start(f32[2,12,192]{2,0,1:T(2,128)S(1)} %copy-done.28), channel_id=1, source_target_pairs={{0,16},{8,24},{16,0},{24,8},{1,17},{9,25},{17,1},{25,9},{2,18},{10... | collective-permute-start | bytes 55304 | tf_op jit(solution)/shard_map/ppermute | solution.py:673
  24.2 15.7 %collective-permute-start.2 = (f32[2,12,192]{2,0,1:T(2,128)S(1)}, f32[2,12,192]{2,0,1:T(2,128)S(1)}, u32[]{:S(2)}, u32[]{:S(2)}) collective-permute-start(f32[2,12,192]{2,0,1:T(2,128)S(1)} %copy-done.28), channel_id=1, source_target_pairs={{0,24},{8,16},{16,8},{24,0},{1,25},{9,17},{17,9},{25,1},{2,26},{10... | collective-permute-start | bytes 55304 | tf_op jit(solution)/shard_map/ppermute | solution.py:673
  34.1 15.5 %all-to-all-start.1 = ((bf16[4,192,640]{2,1,0:T(8,128)(2,1)}), bf16[4,192,640]{2,1,0:T(8,128)(2,1)S(1)}, u32[]{:S(2)}, u32[]{:S(2)}) async-start(bf16[4,192,640]{2,1,0:T(8,128)(2,1)} %get-tuple-element.113), calls=%async_computation.1 | async-start | bytes 1966080 | tf_op jit(solution)/shard_map/all_to_all | solution.py:679
  68.2 29.1 %all-to-all-start.2 = ((bf16[4,6,96,384]{3,2,1,0:T(8,128)(2,1)}), bf16[4,6,96,384]{3,2,1,0:T(8,128)(2,1)S(1)}, u32[]{:S(2)}, u32[]{:S(2)}) async-start(bf16[4,6,96,384]{3,2,1,0:T(8,128)(2,1)} %pick.5), calls=%async_computation.2 | async-start | bytes 3538944 | tf_op jit(solution)/shard_map/all_to_all | solution.py:679
  114.3 89.7 %all-gather.5.cloned.1.call-start = ((), (), s32[]{:S(2)}) async-start(), calls=%async_computation.17 | async-start | bytes 4423680 | tf_op jit(solution)/shard_map/all_gather | solution.py:745
  148.9 19.8 %all-to-all-start.5 = ((bf16[4,192,384]{2,1,0:T(8,128)(2,1)}), bf16[4,192,384]{2,1,0:T(8,128)(2,1)S(1)}, u32[]{:S(2)}, u32[]{:S(2)}) async-start(bf16[4,192,384]{2,1,0:T(8,128)(2,1)} %get-tuple-element.127), calls=%async_computation.5 | async-start | bytes 1179648 | tf_op jit(solution)/shard_map/all_to_all | solution.py:679
  168.7 18.0 %all-to-all-start.6 = ((bf16[4,192,256]{2,1,0:T(8,128)(2,1)}), bf16[4,192,256]{2,1,0:T(8,128)(2,1)S(1)}, u32[]{:S(2)}, u32[]{:S(2)}) async-start(bf16[4,192,256]{2,1,0:T(8,128)(2,1)} %get-tuple-element.132), calls=%async_computation.6 | async-start | bytes 786432 | tf_op jit(solution)/shard_map/all_to_all | solution.py:679
  186.7 12.6 %all-to-all-start.7 = ((bf16[4,192,384]{2,1,0:T(8,128)(2,1)}), bf16[4,192,384]{2,1,0:T(8,128)(2,1)S(1)}, u32[]{:S(2)}, u32[]{:S(2)}) async-start(bf16[4,192,384]{2,1,0:T(8,128)(2,1)} %get-tuple-element.134), calls=%async_computation.7 | async-start | bytes 1179648 | tf_op jit(solution)/shard_map/all_to_all | solution.py:679
  199.3 34.5 %all-to-all-start.8 = ((bf16[4,192,256]{2,1,0:T(8,128)(2,1)}), bf16[4,192,256]{2,1,0:T(8,128)(2,1)S(1)}, u32[]{:S(2)}, u32[]{:S(2)}) async-start(bf16[4,192,256]{2,1,0:T(8,128)(2,1)} %get-tuple-element.144), calls=%async_computation.8 | async-start | bytes 786432 | tf_op jit(solution)/shard_map/all_to_all | solution.py:679
  234.6 21.3 %all-to-all-start.9 = ((bf16[4,384,384]{2,1,0:T(8,128)(2,1)}), bf16[4,384,384]{2,1,0:T(8,128)(2,1)S(1)}, u32[]{:S(2)}, u32[]{:S(2)}) async-start(bf16[4,384,384]{2,1,0:T(8,128)(2,1)} %get-tuple-element.149), calls=%async_computation.9 | async-start | bytes 2359296 | tf_op jit(solution)/shard_map/all_to_all | solution.py:679
  255.9 21.3 %collective-permute-start.4 = (bf16[4,7,96,384]{3,2,1,0:T(8,128)(2,1)}, bf16[4,7,96,384]{3,2,1,0:T(8,128)(2,1)}, u32[]{:S(2)}, u32[]{:S(2)}) collective-permute-start(bf16[4,7,96,384]{3,2,1,0:T(8,128)(2,1)} %get-tuple-element.195), channel_id=1, source_target_pairs={{0,1},{1,0},{2,3},{3,2},{4,5},{5,4},{6,7},{7,6},{8,9},{9,8},{10,11... | collective-permute-start | bytes 6193160 | tf_op jit(solution)/shard_map/ppermute | solution.py:673
  256.0 17.0 %all-to-all-start.10 = ((bf16[4,384,256]{2,1,0:T(8,128)(2,1)}), bf16[4,384,256]{2,1,0:T(8,128)(2,1)S(1)}, u32[]{:S(2)}, u32[]{:S(2)}) async-start(bf16[4,384,256]{2,1,0:T(8,128)(2,1)} %get-tuple-element.157), calls=%async_computation.10 | async-start | bytes 1572864 | tf_op jit(solution)/shard_map/all_to_all | solution.py:679
  273.0 17.0 %all-to-all-start.11 = ((bf16[4,192,384]{2,1,0:T(8,128)(2,1)}), bf16[4,192,384]{2,1,0:T(8,128)(2,1)S(1)}, u32[]{:S(2)}, u32[]{:S(2)}) async-start(bf16[4,192,384]{2,1,0:T(8,128)(2,1)} %get-tuple-element.165), calls=%async_computation.11 | async-start | bytes 1179648 | tf_op jit(solution)/shard_map/all_to_all | solution.py:679
  277.2 81.2 %reduce-scatter.4.cloned.1.call-start = ((), (), s32[]{:S(2)}) async-start(), calls=%async_computation.18 | async-start | bytes 2580480
  290.0 19.6 %all-to-all-start.12 = ((bf16[4,192,256]{2,1,0:T(8,128)(2,1)}), bf16[4,192,256]{2,1,0:T(8,128)(2,1)S(1)}, u32[]{:S(2)}, u32[]{:S(2)}) async-start(bf16[4,192,256]{2,1,0:T(8,128)(2,1)} %get-tuple-element.177), calls=%async_computation.12 | async-start | bytes 786432 | tf_op jit(solution)/shard_map/all_to_all | solution.py:679
  310.3 20.6 %all-to-all-start.13 = ((bf16[4,384,384]{2,1,0:T(8,128)(2,1)}), bf16[4,384,384]{2,1,0:T(8,128)(2,1)S(1)}, u32[]{:S(2)}, u32[]{:S(2)}) async-start(bf16[4,384,384]{2,1,0:T(8,128)(2,1)} %get-tuple-element.187), calls=%async_computation.13 | async-start | bytes 2359296 | tf_op jit(solution)/shard_map/all_to_all | solution.py:679
  333.0 9.3 %collective-permute-start.5 = (bf16[2,96,384]{2,1,0:T(8,128)(2,1)S(1)}, bf16[2,96,384]{2,1,0:T(8,128)(2,1)S(1)}, u32[]{:S(2)}, u32[]{:S(2)}) collective-permute-start(bf16[2,96,384]{2,1,0:T(8,128)(2,1)S(1)} %fusion.4), channel_id=1, source_target_pairs={{0,1},{1,0},{2,3},{3,2},{4,5},{5,4},{6,7},{7,6},{8,9},{9,8},{10,11... | collective-permute-start | bytes 442376 | tf_op jit(solution)/shard_map/ppermute | solution.py:673
  338.8 22.3 %collective-permute-start.10 = (bf16[7,96,384]{2,1,0:T(8,128)(2,1)}, bf16[7,96,384]{2,1,0:T(8,128)(2,1)S(1)}, u32[]{:S(2)}, u32[]{:S(2)}) collective-permute-start(bf16[7,96,384]{2,1,0:T(8,128)(2,1)} %get-tuple-element.263), channel_id=1, source_target_pairs={{0,24},{8,16},{16,8},{24,0},{1,25},{9,17},{17,9},{25,1},{2,26},{10... | collective-permute-start | bytes 1548296 | tf_op jit(solution)/shard_map/ppermute | solution.py:673
  340.3 25.5 %collective-permute-start.8 = (bf16[7,96,384]{2,1,0:T(8,128)(2,1)}, bf16[7,96,384]{2,1,0:T(8,128)(2,1)}, u32[]{:S(2)}, u32[]{:S(2)}) collective-permute-start(bf16[7,96,384]{2,1,0:T(8,128)(2,1)} %get-tuple-element.262), channel_id=1, source_target_pairs={{0,8},{8,0},{16,24},{24,16},{1,9},{9,1},{17,25},{25,17},{2,10},{10... | collective-permute-start | bytes 1548296 | tf_op jit(solution)/shard_map/ppermute | solution.py:673
  341.8 24.0 %collective-permute-start.9 = (bf16[7,96,384]{2,1,0:T(8,128)(2,1)}, bf16[7,96,384]{2,1,0:T(8,128)(2,1)}, u32[]{:S(2)}, u32[]{:S(2)}) collective-permute-start(bf16[7,96,384]{2,1,0:T(8,128)(2,1)} %get-tuple-element.264), channel_id=1, source_target_pairs={{0,16},{8,24},{16,0},{24,8},{1,17},{9,25},{17,1},{25,9},{2,18},{10... | collective-permute-start | bytes 1548296 | tf_op jit(solution)/shard_map/ppermute | solution.py:673
  342.4 30.9 %all-to-all-start.14 = ((bf16[4,384,256]{2,1,0:T(8,128)(2,1)}), bf16[4,384,256]{2,1,0:T(8,128)(2,1)S(1)}, u32[]{:S(2)}, u32[]{:S(2)}) async-start(bf16[4,384,256]{2,1,0:T(8,128)(2,1)} %get-tuple-element.202), calls=%async_computation.14 | async-start | bytes 1572864 | tf_op jit(solution)/shard_map/all_to_all | solution.py:679
  359.6 9.7 %collective-permute-start.6 = (bf16[432,384]{1,0:T(8,128)(2,1)S(1)}, bf16[432,384]{1,0:T(8,128)(2,1)S(1)}, u32[]{:S(2)}, u32[]{:S(2)}) collective-permute-start(bf16[432,384]{1,0:T(8,128)(2,1)S(1)} %constant_dynamic-slice_fusion.3), channel_id=1, source_target_pairs={{0,2},{1,3},{2,0},{3,1},{4,6},{5,7},{6,4},{7,5},{8,10},{9,11},{10,... | collective-permute-start | bytes 995336 | tf_op jit(solution)/shard_map/ppermute | solution.py:673
  367.7 19.6 %collective-permute-start.11 = (bf16[336,384]{1,0:T(8,128)(2,1)S(1)}, bf16[336,384]{1,0:T(8,128)(2,1)S(1)}, u32[]{:S(2)}, u32[]{:S(2)}) collective-permute-start(bf16[336,384]{1,0:T(8,128)(2,1)S(1)} %constant_dynamic-slice_fusion.2), channel_id=1, source_target_pairs={{0,2},{1,3},{2,0},{3,1},{4,6},{5,7},{6,4},{7,5},{8,10},{9,11},{10,... | collective-permute-start | bytes 774152 | tf_op jit(solution)/shard_map/ppermute | solution.py:673
  370.0 17.2 %collective-permute-start.14 = (bf16[432,384]{1,0:T(8,128)(2,1)S(1)}, bf16[432,384]{1,0:T(8,128)(2,1)S(1)}, u32[]{:S(2)}, u32[]{:S(2)}) collective-permute-start(bf16[432,384]{1,0:T(8,128)(2,1)S(1)} %dynamic-slice_add_fusion), channel_id=1, source_target_pairs={{0,4},{1,5},{2,6},{3,7},{4,0},{5,1},{6,2},{7,3},{8,12},{9,13},{10,... | collective-permute-start | bytes 995336 | tf_op jit(solution)/shard_map/ppermute | solution.py:673
  387.4 15.0 %collective-permute-start.12 = (bf16[336,384]{1,0:T(8,128)(2,1)S(1)}, bf16[336,384]{1,0:T(8,128)(2,1)S(1)}, u32[]{:S(2)}, u32[]{:S(2)}) collective-permute-start(bf16[336,384]{1,0:T(8,128)(2,1)S(1)} %dynamic-slice_add_fusion.1), channel_id=1, source_target_pairs={{0,4},{1,5},{2,6},{3,7},{4,0},{5,1},{6,2},{7,3},{8,12},{9,13},{10,... | collective-permute-start | bytes 774152 | tf_op jit(solution)/shard_map/ppermute | solution.py:673
  388.1 18.2 %collective-permute-start.20 = (bf16[432,384]{1,0:T(8,128)(2,1)S(1)}, bf16[432,384]{1,0:T(8,128)(2,1)S(1)}, u32[]{:S(2)}, u32[]{:S(2)}) collective-permute-start(bf16[432,384]{1,0:T(8,128)(2,1)S(1)} %add.267), channel_id=1, source_target_pairs={{0,2},{1,3},{2,0},{3,1},{4,6},{5,7},{6,4},{7,5},{8,10},{9,11},{10,... | collective-permute-start | bytes 995336 | tf_op jit(solution)/shard_map/ppermute | solution.py:673
  390.7 15.5 %collective-permute-start.16 = (bf16[96,384]{1,0:T(8,128)(2,1)S(1)}, bf16[96,384]{1,0:T(8,128)(2,1)S(1)}, u32[]{:S(2)}, u32[]{:S(2)}) collective-permute-start(bf16[96,384]{1,0:T(8,128)(2,1)S(1)} %constant_dynamic-slice_fusion), channel_id=1, source_target_pairs={{0,2},{1,3},{2,0},{3,1},{4,6},{5,7},{6,4},{7,5},{8,10},{9,11},{10,... | collective-permute-start | bytes 221192 | tf_op jit(solution)/shard_map/ppermute | solution.py:673
  402.5 10.1 %collective-permute-start.13 = (bf16[336,384]{1,0:T(8,128)(2,1)S(1)}, bf16[336,384]{1,0:T(8,128)(2,1)S(1)}, u32[]{:S(2)}, u32[]{:S(2)}) collective-permute-start(bf16[336,384]{1,0:T(8,128)(2,1)S(1)} %add.257), channel_id=1, source_target_pairs={{0,2},{1,3},{2,0},{3,1},{4,6},{5,7},{6,4},{7,5},{8,10},{9,11},{10,... | collective-permute-start | bytes 774152 | tf_op jit(solution)/shard_map/ppermute | solution.py:673
  406.5 11.2 %collective-permute-start.21 = (bf16[9,96,384]{2,1,0:T(8,128)(2,1)S(1)}, bf16[9,96,384]{2,1,0:T(8,128)(2,1)S(1)}, u32[]{:S(2)}, u32[]{:S(2)}) collective-permute-start(bf16[9,96,384]{2,1,0:T(8,128)(2,1)S(1)} %bitcast.67), channel_id=1, source_target_pairs={{0,1},{1,0},{2,3},{3,2},{4,5},{5,4},{6,7},{7,6},{8,9},{9,8},{10,11... | collective-permute-start | bytes 1990664 | tf_op jit(solution)/shard_map/ppermute | solution.py:673
  (46 other events, 339.6 us)
Sparse Core Ops, SparseCore 0:
  10.7 54.3 all-gather.2
  123.2 51.6 all-gather.4
  281.0 46.7 reduce-scatter.3
